TPU v7x, 32 devices: a whole 2x2x4 slice. The times are simulated.
32 devices in a mesh: group: 2 (over core), dp: 16 (over z, y, x).
Axes of the slice: x: 2, y: 2, z: 4, core: 2. Of those that a mesh axis runs over, the one named last changes fastest.
Arguments:
- tokens: bfloat16 [2, 16384, 768], P('group', 'dp'), may hold values from -6 to 6
- cotangent: bfloat16 [2, 16384, 768], P('group', 'dp'), may hold values from -6 to 6
- grid_h: int32 [2, 64], P('group', 'dp'), may hold values from 0 to 22, as said below
- grid_w: int32 [2, 64], P('group', 'dp'), may hold values from 0 to 22, as said below
- owner_block: int32 [16], replicated, may hold values from 0 to 15, as said below
- master: float32 [9216, 768], P('dp')
- first_mom: float32 [9216, 768], P('dp'), may hold values from -0.00056339084 to 0.00056339084
- second_mom: float32 [9216, 768], P('dp'), may hold values from 1.4107079e-07 to 5.6428314e-07
- vectors: float32 [14, 768], replicated
- vec_first: float32 [14, 768], replicated, may hold values from -0.0022535634 to 0.0022535634
- vec_second: float32 [14, 768], replicated, may hold values from 2.2571326e-06 to 9.02853e-06
Outputs:
- block_out: bfloat16 [2, 16384, 768], P('group', 'dp')
- input_grad: float32 [2, 16384, 768], P('group', 'dp')
- mat_grad: float32 [9216, 768], P('dp')
- mat_second: float32 [9216, 768], P('dp')
- mat_weight: float32 [9216, 768], P('dp')
- vec_grad: float32 [14, 768], replicated
- vec_second_new: float32 [14, 768], replicated
- vec_weight: float32 [14, 768], replicated
- grad_norm: float32 [], replicated
Inputs may be any that keep to these rules, and one draw needn't show every extreme that they name: `grid_h`: A device's image slots are used from the first on, unused ones (height 0) after them; a device of the first group uses 4 // 2 to 4 slots with sides from 12 to 16; of the second group 4 // 4 to 4 // 2 (at least one) with sides from 16 to 22; heights and widths are drawn independently. `grid_w`: zero exactly where grid_h is zero; otherwise as grid_h. `owner_block`: A permutation of 0 to 16 - 1.
All inputs are finite; a program needn't handle non-finite values.
Results may differ from a plain program's by a relative error of at most 0.02.
Values may be sent and summed in bfloat16 or wider, within the bound.
No kernel may reach another device: no remote copies, remote signals or barrier semaphores. Data moves between devices by JAX's collectives and lax.ppermute only.
A program may use at most 320 MiB of HBM per device.

v0:
```python
import jax
import jax.numpy as jnp
from jax import lax
from jax.sharding import PartitionSpec as P

HEADS = 12
STEP = 7


def place_tokens(heights, widths, count):
    sizes = heights * widths
    ends = jnp.cumsum(sizes)
    starts = ends - sizes
    places = jnp.arange(count, dtype=jnp.int32)
    segment = jnp.sum((places[:, None] >= ends[None, :]).astype(jnp.int32), axis=1)
    slots = jnp.arange(heights.shape[0], dtype=jnp.int32)
    picks = (segment[:, None] == slots[None, :]).astype(jnp.int32)
    begin = jnp.sum(picks * starts[None, :], axis=1)
    across = jnp.maximum(jnp.sum(picks * widths[None, :], axis=1), 1)
    offset = places - begin
    live = places < ends[-1]
    return (segment, offset // across, offset % across, live)


def layer_norm(value, gain, shift):
    centre = value - jnp.mean(value, axis=-1, keepdims=True)
    spread = jnp.mean(centre * centre, axis=-1, keepdims=True)
    return centre * lax.rsqrt(spread + 1e-06) * gain + shift


def rotate(queries, keys_in, freqs, rows_pos, cols_pos):
    heads = queries.shape[1]
    half = queries.shape[2] // 2
    width = freqs.shape[0]
    freq_x = freqs[: width // 2].reshape(heads, half)
    freq_y = freqs[width // 2 :].reshape(heads, half)
    angle = (
        rows_pos.astype(jnp.float32)[:, None, None] * freq_x[None]
        + cols_pos.astype(jnp.float32)[:, None, None] * freq_y[None]
    )
    cosine = jnp.cos(angle)
    sine = jnp.sin(angle)

    def turn(part):
        first = part[..., :half]
        second = part[..., half:]
        return jnp.concatenate(
            [first * cosine - second * sine, first * sine + second * cosine], axis=-1
        )

    return (turn(queries), turn(keys_in))


def gelu_exact(value):
    return jax.nn.gelu(value, approximate=False)


def dot_last(left, right):
    return lax.dot_general(
        left, right, (((1,), (1,)), ((), ())), preferred_element_type=jnp.float32
    )


def dot_rows(left, right):
    return lax.dot_general(
        left, right, (((0,), (0,)), ((), ())), preferred_element_type=jnp.float32
    )


def adam(weight, first, second, grad, rate, decay):
    first_new = 0.5 * first + 0.5 * grad
    second_new = 0.5 * second + 0.5 * grad * grad
    correct = 1.0 - 0.5**STEP
    direction = first_new / correct / (jnp.sqrt(second_new / correct) + 1e-08)
    return (second_new, weight - rate * (direction + decay * weight))


def local(
    tokens,
    cotangent,
    grid_h,
    grid_w,
    owner_block,
    master,
    first_mom,
    second_mom,
    vectors,
    vec_first,
    vec_second,
):
    devices = lax.axis_size("dp")
    count = tokens.shape[1]
    width = tokens.shape[2]
    heads = HEADS
    head_dim = width // heads
    scale = head_dim ** (-0.5)
    segment, rows_pos, cols_pos, live = place_tokens(grid_h[0], grid_w[0], count)
    block_rows = master.shape[0]
    gathered = lax.all_gather(master.astype(jnp.bfloat16), "dp", axis=0, tiled=True)
    inverse = jnp.argsort(owner_block)
    weights = gathered.reshape(devices, block_rows, width)[inverse].reshape(
        devices * block_rows, width
    )
    w_qkv = weights[: 3 * width]
    w_proj = weights[3 * width : 4 * width]
    w_up = weights[4 * width : 8 * width]
    w_down = weights[8 * width :]
    inputs = tokens[0].astype(jnp.float32)
    normed_first, norm_one_back = jax.vjp(layer_norm, inputs, vectors[0], vectors[1])
    first_in = normed_first.astype(jnp.bfloat16)
    qkv_full = dot_last(first_in, w_qkv) + vectors[4:7].reshape(3 * width)
    queries = qkv_full[:, :width].reshape(count, heads, head_dim)
    keys_pre = qkv_full[:, width : 2 * width].reshape(count, heads, head_dim)
    values = qkv_full[:, 2 * width :].reshape(count, heads, head_dim).astype(jnp.bfloat16)

    def turn_pair(query_in, key_in, freqs):
        return rotate(query_in, key_in, freqs, rows_pos, cols_pos)

    (query_rot, key_rot), rotate_back = jax.vjp(turn_pair, queries, keys_pre, vectors[13])
    query_low = query_rot.astype(jnp.bfloat16)
    key_low = key_rot.astype(jnp.bfloat16)
    block = min(512, count)
    block_count = count // block

    def scores_for(index):
        start = index * block
        query_part = lax.dynamic_slice_in_dim(query_low, start, block, 0)
        segment_part = lax.dynamic_slice_in_dim(segment, start, block, 0)
        scores = (
            jnp.einsum("qhd,khd->hqk", query_part, key_low, preferred_element_type=jnp.float32)
            * scale
        )
        same = segment_part[:, None] == segment[None, :]
        return (query_part, jnp.where(same[None], scores, -1000000000.0))

    def attend(index):
        unused_query, scores = scores_for(index)
        top = jnp.max(scores, axis=-1, keepdims=True)
        logsum = top + jnp.log(jnp.sum(jnp.exp(scores - top), axis=-1, keepdims=True))
        probs = jnp.exp(scores - logsum).astype(jnp.bfloat16)
        mixed = jnp.einsum("hqk,khd->qhd", probs, values, preferred_element_type=jnp.float32)
        return (mixed.astype(jnp.bfloat16), logsum)

    mixed_parts, logsums = lax.map(attend, jnp.arange(block_count))
    attn_out = mixed_parts.reshape(count, width)
    middle = inputs + dot_last(attn_out, w_proj) + vectors[7]
    normed_second, norm_two_back = jax.vjp(layer_norm, middle, vectors[2], vectors[3])
    second_in = normed_second.astype(jnp.bfloat16)
    up_pre = dot_last(second_in, w_up) + vectors[8:12].reshape(4 * width)
    activated, gelu_back = jax.vjp(gelu_exact, up_pre)
    hidden = activated.astype(jnp.bfloat16)
    branch_two = jnp.dot(hidden, w_down, preferred_element_type=jnp.float32) + vectors[12]
    block_out = (middle + branch_two).astype(jnp.bfloat16)
    grad_out = cotangent[0].astype(jnp.float32) * live[:, None].astype(jnp.float32)
    grad_two = grad_out.astype(jnp.bfloat16)
    grad_down = dot_rows(hidden, grad_two)
    bias_down = jnp.sum(grad_two.astype(jnp.float32), axis=0)
    grad_hidden = dot_last(grad_two, w_down)
    grad_up_pre = gelu_back(grad_hidden)[0].astype(jnp.bfloat16)
    grad_up = dot_rows(grad_up_pre, second_in)
    bias_up = jnp.sum(grad_up_pre.astype(jnp.float32), axis=0)
    grad_second_in = jnp.dot(grad_up_pre, w_up, preferred_element_type=jnp.float32)
    grad_mid_norm, gain_two, shift_two = norm_two_back(grad_second_in)
    grad_middle = grad_out + grad_mid_norm
    grad_one = grad_middle.astype(jnp.bfloat16)
    grad_proj = dot_rows(grad_one, attn_out)
    bias_proj = jnp.sum(grad_one.astype(jnp.float32), axis=0)
    grad_attn = (
        jnp.dot(grad_one, w_proj, preferred_element_type=jnp.float32)
        .astype(jnp.bfloat16)
        .reshape(count, heads, head_dim)
    )

    def back_step(carry, index):
        grad_keys, grad_values = carry
        query_part, scores = scores_for(index)
        probs = jnp.exp(scores - logsums[index])
        probs_low = probs.astype(jnp.bfloat16)
        grad_part = lax.dynamic_slice_in_dim(grad_attn, index * block, block, 0)
        grad_probs = jnp.einsum(
            "qhd,khd->hqk", grad_part, values, preferred_element_type=jnp.float32
        )
        inner = jnp.sum(probs * grad_probs, axis=-1, keepdims=True)
        grad_scores = (probs * (grad_probs - inner)).astype(jnp.bfloat16)
        grad_query = (
            jnp.einsum("hqk,khd->qhd", grad_scores, key_low, preferred_element_type=jnp.float32)
            * scale
        )
        grad_keys = (
            grad_keys
            + jnp.einsum(
                "hqk,qhd->khd", grad_scores, query_part, preferred_element_type=jnp.float32
            )
            * scale
        )
        grad_values = grad_values + jnp.einsum(
            "hqk,qhd->khd", probs_low, grad_part, preferred_element_type=jnp.float32
        )
        return ((grad_keys, grad_values), grad_query)

    zero_heads = jnp.zeros((count, heads, head_dim), jnp.float32)
    (grad_keys, grad_values), grad_queries = lax.scan(
        back_step, (zero_heads, zero_heads), jnp.arange(block_count)
    )
    grad_queries = grad_queries.reshape(count, heads, head_dim)
    grad_q_pre, grad_k_pre, grad_freqs = rotate_back((grad_queries, grad_keys))
    grad_qkv = jnp.concatenate(
        [
            grad_q_pre.reshape(count, width),
            grad_k_pre.reshape(count, width),
            grad_values.reshape(count, width),
        ],
        axis=1,
    ).astype(jnp.bfloat16)
    grad_qkv_w = dot_rows(grad_qkv, first_in)
    bias_qkv = jnp.sum(grad_qkv.astype(jnp.float32), axis=0).reshape(3, width)
    grad_first_in = jnp.dot(grad_qkv, w_qkv, preferred_element_type=jnp.float32)
    grad_in_norm, gain_one, shift_one = norm_one_back(grad_first_in)
    input_grad = grad_middle + grad_in_norm
    local_vec = jnp.concatenate(
        [
            gain_one[None],
            shift_one[None],
            gain_two[None],
            shift_two[None],
            bias_qkv,
            bias_proj[None],
            bias_up.reshape(4, width),
            bias_down[None],
            grad_freqs[None],
        ],
        axis=0,
    )
    local_mat = jnp.concatenate([grad_qkv_w, grad_proj, grad_up, grad_down], axis=0)
    owner_term = local_mat.reshape(devices, block_rows, width)[owner_block].reshape(
        devices * block_rows, width
    )
    share = lax.psum_scatter(owner_term, "dp", scatter_dimension=0, tiled=True)
    share = lax.psum(share.astype(jnp.bfloat16), "group").astype(jnp.float32)
    vec_total = lax.psum(local_vec, ("group", "dp"))
    square = lax.psum(jnp.sum(share * share), "dp")
    grad_norm = jnp.sqrt(square + jnp.sum(vec_total * vec_total))
    clip = jnp.minimum(1.0, 1.0 / (grad_norm + 1e-06))
    mat_grad = share * clip
    vec_grad = vec_total * clip
    mat_second, mat_weight = adam(master, first_mom, second_mom, mat_grad, 0.02, 0.05)
    vec_second_new, vec_weight = adam(vectors, vec_first, vec_second, vec_grad, 0.2, 0.0)
    return (
        block_out[None],
        input_grad[None],
        mat_grad,
        mat_second,
        mat_weight,
        vec_grad,
        vec_second_new,
        vec_weight,
        grad_norm,
    )


def solution(mesh):
    return jax.shard_map(
        local,
        mesh=mesh,
        in_specs=(
            P("group", "dp", None),
            P("group", "dp", None),
            P("group", "dp"),
            P("group", "dp"),
            P(),
            P("dp", None),
            P("dp", None),
            P("dp", None),
            P(),
            P(),
            P(),
        ),
        out_specs=(
            P("group", "dp", None),
            P("group", "dp", None),
            P("dp", None),
            P("dp", None),
            P("dp", None),
            P(),
            P(),
            P(),
            P(),
        ),
        check_vma=False,
    )
```

profile of v0, /device:TPU:0, one launch (start us, length us, event | category | flops | bytes accessed | tf_op | source)
XLA Modules:
  0.0 1210.7 jit_solution(16470790264255114463)
XLA Ops:
  20.5 160.5 %all-gather.2.cloned.1.call-done = bf16[9216,768]{1,0:T(8,128)(2,1)} async-done(((bf16[576,768]{1,0:T(8,128)(2,1)}), bf16[9216,768]{1,0:T(8,128)(2,1)}) %all-gather.2.cloned.1.call-update) | async-done | bytes 14155792 | tf_op jit(solution)/shard_map/all_gather | solution.py:99
  181.0 12.1 gather_fusion
  223.2 76.1 %while.27 = (s32[]{:T(128)}, bf16[2,512,12,64]{1,3,2,0:T(8,128)(2,1)}, f32[2,12,512,1]{2,1,3,0:T(8,128)S(1)}, s32[2]{0:T(128)S(1)}, s32[1024]{0:T(1024)S(1)}, /*...) while((s32[]{:T(128)}, ...), condition=%wide.region_10.11_spmd, body=%wide.region_7.10_spmd.sunk | while | flops 1680730112 | bytes 95144192 | solution.py:144
  225.1 12.0 fusion.153
  237.1 11.9 exponential_reduce_fusion.2
  263.1 12.0 fusion.153
  275.1 11.9 exponential_reduce_fusion.2
  308.7 38.0 %multiply_convert_fusion.1 = (bf16[1024,3072]{1,0:T(8,128)(2,1)}, f32[1024,3072]{1,0:T(8,128)}, f32[1024,3072]{1,0:T(8,128)}) fusion(f32[3072]{0:T(1024)S(1)} %copy-done.67, bf16[9216,768]{1,0:T(8,128)(2,1)} %bitcast.160, f32[1024,768]{0,1:T(8,128)S(1)} %get-tuple-element.289, f32[768]{0:T(1024)S(1)} %copy-done.72, f32[768]{0:T(1024)S(1)} %copy-done.62, ...), kind=kOutput, calls=%fused_computation.47 | convolution fusion | flops 5043388416 | bytes 39348224 | tf_op jit(solution)/shard_map/dot_general | solution.py:59
  346.6 17.7 %convert_reduce_fusion = (f32[3072]{0:T(1024)}, bf16[1024,3072]{1,0:T(8,128)(2,1)}) fusion(f32[1024,3072]{1,0:T(8,128)} %get-tuple-element.267, bf16[9216,768]{1,0:T(8,128)(2,1)} %bitcast.161, bf16[1,1024,768]{1,2,0:T(8,128)(2,1)S(1)} %copy-done.12, f32[1024]{0:T(1024)S(1)} %copy-done.52, f32[1024,3072]{1,0:T(8,128)} %get-tuple-element.290, ...), kind=kOutput, calls=%fused_computation.45 | convolution fusion | flops 4887671808 | bytes 37777408 | tf_op jit(solution)/shard_map/dot_general | solution.py:59
  399.6 236.9 %while.28 = (s32[]{:T(128)}, f32[1024,12,64]{0,2,1:T(8,128)}, f32[1024,12,64]{0,2,1:T(8,128)}, f32[2,512,12,64]{1,0,3,2:T(2,128)}, s32[2]{0:T(128)S(1)}, /*index...) while((s32[]{:T(128)}, f32[1024,12,64]{0,2,1:T(8,128)}, ...), condition=%wide.region_17.18_spmd.clone, body=%wide.region_15.17_spmd.clone.sunk | while | flops 4125747200 | bytes 250800496 | solution.py:202
  415.0 18.1 %multiply_reduce_fusion.8 = (f32[12,512]{1,0:T(8,128)S(1)}, f32[12,512,1024]{2,1,0:T(8,128)}) fusion(f32[12,512,1024]{2,1,0:T(8,128)} %fusion.164, f32[12,512]{1,0:T(8,128)S(1)} %dynamic-slice_bitcast_fusion.2, pred[512,1024]{1,0:T(8,128)(4,1)S(1)} %broadcast_compare_fusion.5, bf16[1024,12,64]{0,2,1:T(8,128)(2,1)} %get-tuple-element.505, ...), kind=kOutput, calls=%fused_computation.20.clone.1 | convolution fusion | flops 836757504 | bytes 53264388 | tf_op jit(solution)/shard_map/while/body/eval_jaxpr/qhd,khd->hqk/dot_general | solution.py:180
  433.1 21.2 %multiply_convert_fusion.3 = bf16[12,512,1024]{2,1,0:T(8,128)(2,1)} fusion(f32[12,512,1024]{2,1,0:T(8,128)} %get-tuple-element.425, f32[12,512,1024]{2,1,0:T(8,128)} %fusion.164, f32[12,512]{1,0:T(8,128)S(1)} %get-tuple-element.426, f32[12,512]{1,0:T(8,128)S(1)} %dynamic-slice_bitcast_fusion.2, pred[512,1024]{1,0:T(8,128)(4,1)S(1)} %broadcast_compare_fusion.5), kind=kLoop, calls=%fused_computation.19.clone.1 | loop fusion | flops 37748736 | bytes 63488000 | tf_op jit(solution)/shard_map/while/body/eval_jaxpr/convert_element_type | solution.py:184
  463.2 11.5 bitcast_add_fusion.5
  489.1 28.7 %dynamic_update_slice.20 = f32[2,512,12,64]{1,0,3,2:T(2,128)} dynamic-update-slice(f32[2,512,12,64]{1,0,3,2:T(2,128)} %get-tuple-element.482, f32[1,512,12,64]{1,0,3,2:T(1,128)S(1)} %copy.94, s32[]{:T(128)S(6)} %copy.111, s32[]{:T(128)} %constant.36.clone.1..sunk.1, s32[]{:T(128)} %constant.36.clone.1..sunk.1, s32[]{:T(128)} %constant.36.clone.1..sunk.1) | dynamic-update-slice | bytes 3145732 | tf_op jit(solution)/shard_map/while/body/jit(dynamic_update_index_in_dim)/dynamic_update_slice | solution.py:202
  532.7 18.1 %multiply_reduce_fusion.8 = (f32[12,512]{1,0:T(8,128)S(1)}, f32[12,512,1024]{2,1,0:T(8,128)}) fusion(f32[12,512,1024]{2,1,0:T(8,128)} %fusion.164, f32[12,512]{1,0:T(8,128)S(1)} %dynamic-slice_bitcast_fusion.2, pred[512,1024]{1,0:T(8,128)(4,1)S(1)} %broadcast_compare_fusion.5, bf16[1024,12,64]{0,2,1:T(8,128)(2,1)} %get-tuple-element.505, ...), kind=kOutput, calls=%fused_computation.20.clone.1 | convolution fusion | flops 836757504 | bytes 53264388 | tf_op jit(solution)/shard_map/while/body/eval_jaxpr/qhd,khd->hqk/dot_general | solution.py:180
  550.8 21.2 %multiply_convert_fusion.3 = bf16[12,512,1024]{2,1,0:T(8,128)(2,1)} fusion(f32[12,512,1024]{2,1,0:T(8,128)} %get-tuple-element.425, f32[12,512,1024]{2,1,0:T(8,128)} %fusion.164, f32[12,512]{1,0:T(8,128)S(1)} %get-tuple-element.426, f32[12,512]{1,0:T(8,128)S(1)} %dynamic-slice_bitcast_fusion.2, pred[512,1024]{1,0:T(8,128)(4,1)S(1)} %broadcast_compare_fusion.5), kind=kLoop, calls=%fused_computation.19.clone.1 | loop fusion | flops 37748736 | bytes 63488000 | tf_op jit(solution)/shard_map/while/body/eval_jaxpr/convert_element_type | solution.py:184
  581.8 11.5 bitcast_add_fusion.5
  607.7 28.7 %dynamic_update_slice.20 = f32[2,512,12,64]{1,0,3,2:T(2,128)} dynamic-update-slice(f32[2,512,12,64]{1,0,3,2:T(2,128)} %get-tuple-element.482, f32[1,512,12,64]{1,0,3,2:T(1,128)S(1)} %copy.94, s32[]{:T(128)S(6)} %copy.111, s32[]{:T(128)} %constant.36.clone.1..sunk.1, s32[]{:T(128)} %constant.36.clone.1..sunk.1, s32[]{:T(128)} %constant.36.clone.1..sunk.1) | dynamic-update-slice | bytes 3145732 | tf_op jit(solution)/shard_map/while/body/jit(dynamic_update_index_in_dim)/dynamic_update_slice | solution.py:202
  645.6 12.1 multiply_add_fusion.1
  681.5 24.6 %pad_maximum_fusion = f32[9216,768]{1,0:T(8,128)} fusion(f32[3072,768]{1,0:T(8,128)S(1)} %fusion.89, f32[3072,768]{1,0:T(8,128)S(1)} %bitcast.168, f32[768,768]{1,0:T(8,128)} %fusion.119, f32[2304,768]{1,0:T(8,128)} %fusion.74), kind=kLoop, calls=%fused_computation.42 | loop fusion | flops 21233664 | bytes 56623104 | tf_op jit(solution)/shard_map/concatenate | solution.py:234
  706.1 21.0 %gather_fusion.1 = f32[16,576,768]{2,1,0:T(8,128)} fusion(f32[16,576,768]{2,1,0:T(8,128)} %bitcast.153, s32[1024]{0:T(1024)} %pad_clamp_fusion), kind=kCustom, calls=%fused_computation.1 | custom fusion | bytes 56623168 | tf_op jit(solution)/shard_map/gather | solution.py:235
  745.8 43.8 %psum.23 = f32[14,768]{1,0:T(8,128)S(1)} all-reduce(f32[14,768]{1,0:T(8,128)S(1)} %concatenate.22), channel_id=1, replica_groups=mesh['group'=2,'dp'=16] {'group','dp'}, use_global_device_ids=true, to_apply=%region_34.35 | all-reduce | flops 10752 | bytes 86016 | tf_op jit(solution)/shard_map/psum | solution.py:240
  799.8 325.8 %reduce-scatter.2.cloned.1.call-done = f32[576,768]{1,0:T(8,128)} async-done(((f32[9216,768]{1,0:T(8,128)}), f32[576,768]{1,0:T(8,128)}) %reduce-scatter.2.cloned.1.call-update) | async-done | bytes 1769488 | tf_op jit(solution)/shard_map/reduce_scatter | solution.py:238
  1153.0 42.6 %psum.22 = f32[]{:T(128)} all-reduce(f32[]{:T(128)} %fusion.63), channel_id=1, replica_groups=mesh['group'=2,'dp'=16] {'dp'}, use_global_device_ids=true, to_apply=%region_23.24 | all-reduce | flops 1 | bytes 8 | tf_op jit(solution)/shard_map/psum | solution.py:241
  (304 shorter events, 280.6 us)
Async XLA Ops:
  7.2 173.8 %all-gather.2.cloned.1.call-start = ((), (), s32[]{:S(2)}) async-start(), calls=%async_computation.1 | async-start | bytes 15040512 | tf_op jit(solution)/shard_map/all_gather | solution.py:99
  9.9 1115.7 %reduce-scatter.2.cloned.1.call-start = ((), (), s32[]{:S(2)}) async-start(), calls=%async_computation.2 | async-start | bytes 30081024 | tf_op jit(solution)/shard_map/reduce_scatter | solution.py:238
  11.0 184.4 %copy-start.4 = (bf16[1,1024,768]{1,2,0:T(8,128)(2,1)}, bf16[1,1024,768]{1,2,0:T(8,128)(2,1)S(1)}, u32[]{:S(2)}) copy-start(bf16[1,1024,768]{1,2,0:T(8,128)(2,1)S(1)} %copy.49) | copy-start | bytes 4718596
  11.1 199.6 %copy-start.38 = (f32[12,32]{1,0:T(8,128)}, f32[12,32]{1,0:T(8,128)S(1)}, u32[]{:S(2)}) copy-start(f32[12,32]{1,0:T(8,128)S(1)} %mul.433) | copy-start | bytes 4612
  11.2 199.5 %copy-start.40 = (f32[12,32]{1,0:T(8,128)}, f32[12,32]{1,0:T(8,128)S(1)}, u32[]{:S(2)}) copy-start(f32[12,32]{1,0:T(8,128)S(1)} %mul.429) | copy-start | bytes 4612
  19.0 176.4 %copy-start.44 = (f32[768]{0:T(1024)}, f32[768]{0:T(1024)S(1)}, u32[]{:S(2)}) copy-start(f32[768]{0:T(1024)S(1)} %get-tuple-element.210) | copy-start | bytes 9220
  19.0 176.4 %copy-start.70 = (f32[768]{0:T(1024)}, f32[768]{0:T(1024)S(1)}, u32[]{:S(2)}) copy-start(f32[768]{0:T(1024)S(1)} %get-tuple-element.209) | copy-start | bytes 9220
  19.3 176.1 %copy-start.42 = (f32[1024]{0:T(1024)}, f32[1024]{0:T(1024)S(1)}, u32[]{:S(2)}) copy-start(f32[1024]{0:T(1024)S(1)} %broadcast_multiply_fusion.2) | copy-start | bytes 12292
  19.8 175.6 %copy-start.54 = (f32[1024]{0:T(1024)}, f32[1024]{0:T(1024)S(1)}, u32[]{:S(2)}) copy-start(f32[1024]{0:T(1024)S(1)} %fusion.105) | copy-start | bytes 12292
  20.5 190.3 %copy-start.46 = (f32[1024]{0:T(1024)}, f32[1024]{0:T(1024)S(1)}, u32[]{:S(2)}) copy-start(f32[1024]{0:T(1024)S(1)} %get-tuple-element.286) | copy-start | bytes 12292
  20.5 190.3 %copy-start.48 = (f32[1024]{0:T(1024)}, f32[1024]{0:T(1024)S(1)}, u32[]{:S(2)}) copy-start(f32[1024]{0:T(1024)S(1)} %get-tuple-element.287) | copy-start | bytes 12292
  237.1 11.9 copy-start.28
  307.3 82.7 %copy-start.9 = (f32[1024,768]{0,1:T(8,128)}, f32[1024,768]{0,1:T(8,128)S(1)}, u32[]{:S(2)}) copy-start(f32[1024,768]{0,1:T(8,128)S(1)} %get-tuple-element.289) | copy-start | bytes 9437188
  308.7 38.0 %copy-start.12 = (bf16[1,1024,768]{1,2,0:T(8,128)(2,1)S(1)}, bf16[1,1024,768]{1,2,0:T(8,128)(2,1)}, u32[]{:S(2)}) copy-start(bf16[1,1024,768]{1,2,0:T(8,128)(2,1)} %copy.55) | copy-start | bytes 4718596
  308.7 38.0 %copy-start.52 = (f32[1024]{0:T(1024)S(1)}, f32[1024]{0:T(1024)}, u32[]{:S(2)}) copy-start(f32[1024]{0:T(1024)} %fusion.104) | copy-start | bytes 12292
  645.6 12.1 copy-start.8
  727.1 419.9 %all-reduce.8.cloned.1.call-start = ((), (), s32[]{:S(2)}) async-start(), calls=%async_computation.3 | async-start | bytes 1769472 | tf_op jit(solution)/shard_map/psum | solution.py:239
  743.9 45.7 %copy-start.69 = (f32[768]{0:T(1024)S(1)}, f32[768]{0:T(1024)}, u32[]{:S(2)}) copy-start(f32[768]{0:T(1024)} %get-tuple-element.211) | copy-start | bytes 9220
  799.8 331.5 %copy-start.57 = (f32[1024]{0:T(1024)S(1)}, f32[1024]{0:T(1024)}, u32[]{:S(2)}) copy-start(f32[1024]{0:T(1024)} %copy-done.56) | copy-start | bytes 12292
  1149.3 47.7 %copy-start.37 = (f32[14,768]{1,0:T(8,128)S(1)}, f32[14,768]{1,0:T(8,128)}, u32[]{:S(2)}) copy-start(f32[14,768]{1,0:T(8,128)} %param.23) | copy-start | bytes 129028
  1149.3 47.7 %copy-start.50 = (f32[14,768]{1,0:T(8,128)S(1)}, f32[14,768]{1,0:T(8,128)}, u32[]{:S(2)}) copy-start(f32[14,768]{1,0:T(8,128)} %param.24) | copy-start | bytes 129028
  1149.3 47.7 %copy-start.51 = (f32[14,768]{1,0:T(8,128)S(1)}, f32[14,768]{1,0:T(8,128)}, u32[]{:S(2)}) copy-start(f32[14,768]{1,0:T(8,128)} %param.25) | copy-start | bytes 129028
  1149.3 48.4 %copy-start.16 = (f32[576,768]{1,0:T(8,128)S(1)}, f32[576,768]{1,0:T(8,128)}, u32[]{:S(2)}) copy-start(f32[576,768]{1,0:T(8,128)} %param.20) | copy-start | bytes 5308420
  1149.3 48.4 %copy-start.23 = (bf16[576,768]{1,0:T(8,128)(2,1)S(1)}, bf16[576,768]{1,0:T(8,128)(2,1)}, u32[]{:S(2)}) copy-start(bf16[576,768]{1,0:T(8,128)(2,1)} %all-reduce.8.cloned.1.call-done) | copy-start | bytes 2654212
  (66 other events, 256.5 us)
Sparse Core Ops, SparseCore 0:
  11.4 169.5 all-gather.1
  727.2 398.3 reduce-scatter.1
  1128.5 18.4 all-reduce.7
where the time goes:
time: 1220 us; the launch traced here: 1210 us
  waiting for transfers between devices  496 us (41%)
  matrix products  288 us (24%)
  other arithmetic  162 us (13%)
  local copies, waits for them, and re-layouts  153 us (13%)
  blocking collectives  86.4 us (7%)
  between operations  17.8 us (1%)
    reduce_scatter x1, waiting for transfers between devices, local(): share = lax.psum_scatter(owner_term, 'dp', scatter_dimension=0, tiled=True)  326 us
    all_gather x1, waiting for transfers between devices, local(): lax.all_gather(master.astype(jnp.bfloat16), 'dp', axis=0, tiled=True)  161 us
    dynamic_update_slice x4, local copies, waits for them, and re-layouts, local(): lax.scan(back_step, (zero_heads, zero_heads), jnp.arange(block_count))  63.4 us
    dot_general x4, matrix products, dot_last(): lax.dot_general(left, right, (((1,), (1,)), ((), ())), preferred_element_...  63.3 us
    dot_general x4, matrix products, scores_for(): jnp.einsum('qhd,khd->hqk', query_part, key_low, preferred_element_type=jn...  46.5 us
    psum x1, blocking collectives, local(): vec_total = lax.psum(local_vec, ('group', 'dp'))  43.8 us
    psum x1, blocking collectives, local(): square = lax.psum(jnp.sum(share * share), 'dp')  42.6 us
    convert_element_type x2, other arithmetic, back_step(): grad_scores = (probs * (grad_probs - inner)).astype(jnp.bfloat16)  42.4 us
  transfers between devices with their start and end apart: 3, of which 3 were waited for; matrix products, arithmetic and copies ran while one was open for 4% of the time, Pallas kernels for 0%

commit v1 on v0

v1 whole, which is shorter than its diff:
```python
import functools
import jax
import jax.numpy as jnp
from jax import lax
from jax.experimental import pallas as pl
from jax.experimental.pallas import tpu as pltpu

F32 = jnp.float32
BF16 = jnp.bfloat16
LAST = (((1,), (1,)), ((), ()))
FIRST = (((0,), (0,)), ((), ()))
PLAIN = (((1,), (0,)), ((), ()))
MASKED = -1e9


def mm(left, right, dims):
    return lax.dot_general(left, right, dims, preferred_element_type=F32)


def norm_parts(value):
    centre = value - jnp.mean(value, axis=-1, keepdims=True)
    spread = jnp.mean(centre * centre, axis=-1, keepdims=True)
    inverse = lax.rsqrt(spread + 1e-6)
    return centre * inverse, inverse


def norm_back(unit, inverse, grad, gain):
    scaled = grad * gain
    first = jnp.mean(scaled, axis=-1, keepdims=True)
    second = jnp.mean(scaled * unit, axis=-1, keepdims=True)
    return inverse * (scaled - first - unit * second)


def swap_halves(value):
    lane = lax.broadcasted_iota(jnp.int32, value.shape, 1)
    return jnp.where(
        lane % 64 < 32, pltpu.roll(value, 96, 1), pltpu.roll(value, 32, 1)
    )


def split3(value):
    one = value.astype(BF16).astype(F32)
    rest = value - one
    two = rest.astype(BF16).astype(F32)
    return one, two, rest - two


def attend_kernel(x_ref, g_ref, b_ref, wq_ref, wk_ref, wv_ref, bq_ref, bk_ref, bv_ref,
                  cos_ref, sin_ref, qm_ref, km_ref,
                  n1_ref, q_ref, k_ref, v_ref, attn_ref, stat_ref, n1_s):
    count = x_ref.shape[0]

    @pl.when(pl.program_id(0) == 0)
    def _():
        unit, _ = norm_parts(x_ref[...].astype(F32))
        n1 = (unit * g_ref[...] + b_ref[...]).astype(BF16)
        n1_s[...] = n1
        n1_ref[...] = n1

    w = jnp.concatenate([wq_ref[...], wk_ref[...], wv_ref[...]], axis=0)
    qkv = mm(n1_s[...], w, LAST)
    q = qkv[:, :128] + bq_ref[...]
    k = qkv[:, 128:256] + bk_ref[...]
    v = (qkv[:, 256:] + bv_ref[...]).astype(BF16)
    c = cos_ref[...]
    s = sin_ref[...]
    qr = ((q * c + swap_halves(q) * s).astype(BF16).astype(F32) * 0.125).astype(BF16)
    kr = (k * c + swap_halves(k) * s).astype(BF16)
    q_ref[...] = qr
    k_ref[...] = kr
    v_ref[...] = v
    lane = lax.broadcasted_iota(jnp.int32, (1, 128), 1)
    k_aug = jnp.concatenate([kr, km_ref[...]], axis=1)
    v_aug = jnp.concatenate([v, jnp.ones((count, 128), BF16)], axis=1)
    zero = jnp.zeros((), BF16)
    tile = 256
    for i in range(count // tile):
        rows = pl.ds(i * tile, tile)
        out = None
        stats = []
        for h in (0, 1):
            mine = (lane // 64) == h
            qa = jnp.concatenate(
                [jnp.where(mine, qr[i * tile:(i + 1) * tile], zero), qm_ref[rows, :]], axis=1)
            scores = mm(qa, k_aug, LAST)
            top = jnp.max(scores, axis=-1, keepdims=True)
            e = jnp.exp(scores - top).astype(BF16)
            o = mm(e, v_aug, PLAIN)
            total = o[:, 128:]
            o = o[:, :128] / total
            out = o if out is None else jnp.where(lane < 64, out, o)
            stats.append(top + jnp.log(total[:, :1]))
        attn_ref[rows, :] = out.astype(BF16)
        stat_ref[rows, :] = jnp.where(lane < 64, stats[0], stats[1])


def attend(x, gain, shift, wqkv, bqkv, cos, sin, qm, km):
    count, width = x.shape
    pairs = width // 128
    whole = lambda p: (0, 0)
    col = lambda p: (0, p)
    specs = [
        pl.BlockSpec((count, width), whole),
        pl.BlockSpec((1, width), whole),
        pl.BlockSpec((1, width), whole),
        pl.BlockSpec((128, width), lambda p: (p, 0)),
        pl.BlockSpec((128, width), lambda p: (p + pairs, 0)),
        pl.BlockSpec((128, width), lambda p: (p + 2 * pairs, 0)),
        pl.BlockSpec((1, 128), col),
        pl.BlockSpec((1, 128), lambda p: (0, p + pairs)),
        pl.BlockSpec((1, 128), lambda p: (0, p + 2 * pairs)),
        pl.BlockSpec((count, 128), col),
        pl.BlockSpec((count, 128), col),
        pl.BlockSpec((count, 128), whole),
        pl.BlockSpec((count, 128), whole),
    ]
    outs = [pl.BlockSpec((count, width), whole)] + [pl.BlockSpec((count, 128), col)] * 5
    shape = lambda d: jax.ShapeDtypeStruct((count, width), d)
    return pl.pallas_call(
        attend_kernel,
        grid=(pairs,),
        in_specs=specs,
        out_specs=outs,
        out_shape=[shape(BF16)] * 5 + [shape(F32)],
        scratch_shapes=[pltpu.VMEM((count, width), BF16)],
        compiler_params=pltpu.CompilerParams(vmem_limit_bytes=56 * 2**20),
        name="attend",
    )(x, gain, shift, wqkv, wqkv, wqkv, bqkv, bqkv, bqkv, cos, sin, qm, km)


HALF_ERFC = (
    0.09317889578353007, 0.09147806194869737, 0.10061136147272338, 0.023612303617162326,
    0.20424612730309272, -0.1755704972361086, 0.23011593265708702, -0.06767218931083122,
)


def gelu_both(x):
    e = jnp.exp(x * x * -0.5)
    d = jnp.abs(x) * (0.33 * 0.7071067811865476) + 1.0
    t = pl.reciprocal(d, approx=True)
    t = t * (2.0 - d * t)
    poly = jnp.full_like(t, HALF_ERFC[-1])
    for c in HALF_ERFC[-2::-1]:
        poly = poly * t + c
    tail = poly * t * e
    cdf = jnp.where(x >= 0, 1.0 - tail, tail)
    return x * cdf, cdf + x * e * 0.3989422804014327


def mlp_kernel(n2_ref, dz_ref, w1_ref, w2_ref, b1_ref, out_ref, dn_ref, g1_ref, g2_ref, gb_ref):
    @pl.when(pl.program_id(0) == 0)
    def _():
        out_ref[...] = jnp.zeros_like(out_ref)
        dn_ref[...] = jnp.zeros_like(dn_ref)

    n2 = n2_ref[...]
    dz = dz_ref[...]
    w1 = w1_ref[...]
    w2 = w2_ref[...]
    pre = mm(n2, w1, LAST) + b1_ref[...]
    act, slope = gelu_both(pre)
    hidden = act.astype(BF16)
    out_ref[...] += mm(hidden, w2, PLAIN)
    g2_ref[...] = mm(hidden, dz, FIRST).astype(BF16)
    dpre = (mm(dz, w2, LAST) * slope).astype(BF16)
    gb_ref[...] = jnp.sum(dpre.astype(F32), axis=0, keepdims=True)
    g1_ref[...] = mm(dpre, n2, FIRST).astype(BF16)
    dn_ref[...] += mm(dpre, w1, PLAIN)


def mlp(n2, dz, w1, w2, b1, tile=256):
    count, width = n2.shape
    units = w1.shape[0]
    whole = lambda t: (0, 0)
    row = lambda t: (t, 0)
    return pl.pallas_call(
        mlp_kernel,
        grid=(units // tile,),
        in_specs=[
            pl.BlockSpec((count, width), whole),
            pl.BlockSpec((count, width), whole),
            pl.BlockSpec((tile, width), row),
            pl.BlockSpec((tile, width), row),
            pl.BlockSpec((1, tile), lambda t: (0, t)),
        ],
        out_specs=[
            pl.BlockSpec((count, width), whole),
            pl.BlockSpec((count, width), whole),
            pl.BlockSpec((tile, width), row),
            pl.BlockSpec((tile, width), row),
            pl.BlockSpec((1, tile), lambda t: (0, t)),
        ],
        out_shape=[
            jax.ShapeDtypeStruct((count, width), F32),
            jax.ShapeDtypeStruct((count, width), F32),
            jax.ShapeDtypeStruct((units, width), BF16),
            jax.ShapeDtypeStruct((units, width), BF16),
            jax.ShapeDtypeStruct((1, units), F32),
        ],
        compiler_params=pltpu.CompilerParams(vmem_limit_bytes=56 * 2**20),
        name="mlp",
    )(n2, dz, w1, w2, b1)


def back_kernel(q_ref, k_ref, v_ref, da_ref, at_ref, stat_ref, cos_ref, sin_ref, qm_ref, km_ref,
                pos_ref, n1_ref, wq_ref, wk_ref, wv_ref,
                gq_ref, gk_ref, gv_ref, gb_ref, gf_ref, dn_ref):
    count = q_ref.shape[0]

    @pl.when(pl.program_id(0) == 0)
    def _():
        dn_ref[...] = jnp.zeros_like(dn_ref)

    lane = lax.broadcasted_iota(jnp.int32, (1, 128), 1)
    zero = jnp.zeros((), BF16)
    q = q_ref[...]
    k = k_ref[...]
    v = v_ref[...]
    da = da_ref[...]
    prod = da.astype(F32) * at_ref[...].astype(F32)
    qm = qm_ref[...]
    k_aug = jnp.concatenate([k, km_ref[...]], axis=1)
    v_aug = jnp.concatenate([v, jnp.broadcast_to((lane < 2).astype(BF16), (count, 128))], axis=1)
    tile = 256
    dq = dk = dv = None
    for h in (0, 1):
        mine = (lane // 64) == h
        qh = jnp.where(mine, q, zero)
        kh = jnp.where(mine, k, zero)
        dah = jnp.where(mine, da, zero)
        delta = jnp.sum(jnp.where(mine, prod, 0.0), axis=-1, keepdims=True)
        d1, d2, _ = split3(delta)
        l1, l2, l3 = split3(stat_ref[:, 64 * h:64 * h + 1])
        q_aug = jnp.concatenate(
            [qh, jnp.where(lane == 8, -l1, jnp.where(lane == 9, -l2, jnp.where(lane == 10, -l3, qm.astype(F32)))).astype(BF16)], axis=1)
        da_aug = jnp.concatenate(
            [dah, jnp.where(lane == 0, -d1, jnp.where(lane == 1, -d2, 0.0)).astype(BF16)], axis=1)
        dks, dvs, dqh = [], [], None
        for i in range(count // tile):
            sl = slice(i * tile, (i + 1) * tile)
            p = jnp.exp(mm(k_aug[sl], q_aug, LAST))
            pl_low = p.astype(BF16)
            dp = mm(v_aug[sl], da_aug, LAST)
            ds = (p * dp).astype(BF16)
            dvs.append(mm(pl_low, dah, PLAIN))
            dks.append(mm(ds, qh, PLAIN))
            part = mm(ds, kh[sl], FIRST)
            dqh = part if dqh is None else dqh + part
        dkh = jnp.concatenate(dks, axis=0)
        dvh = jnp.concatenate(dvs, axis=0)
        dq = dqh if dq is None else dq + dqh
        dk = dkh if dk is None else dk + dkh
        dv = dvh if dv is None else dv + dvh
    dq = dq * 0.125
    c = cos_ref[...]
    s = sin_ref[...]
    turned = dq * swap_halves(q.astype(F32) * 8.0) + dk * swap_halves(k.astype(F32))
    turned = jnp.where(lane % 64 < 32, -turned, turned)
    gf_ref[...] = jnp.concatenate(
        [jnp.sum(turned * pos_ref[:, 0:1], axis=0, keepdims=True),
         jnp.sum(turned * pos_ref[:, 1:2], axis=0, keepdims=True)] + [jnp.zeros((6, 128), F32)], axis=0)
    dqp = (dq * c - swap_halves(dq) * s).astype(BF16)
    dkp = (dk * c - swap_halves(dk) * s).astype(BF16)
    dvp = dv.astype(BF16)
    row = lambda a: jnp.sum(a.astype(F32), axis=0, keepdims=True)
    gb_ref[...] = jnp.concatenate([row(dqp), row(dkp), row(dvp), jnp.zeros((5, 128), F32)], axis=0)
    d = jnp.concatenate([dqp, dkp, dvp], axis=1)
    w = jnp.concatenate([wq_ref[...], wk_ref[...], wv_ref[...]], axis=0)
    dn_ref[...] += mm(d, w, PLAIN)
    g = mm(d, n1_ref[...], FIRST).astype(BF16)
    gq_ref[...] = g[:128]
    gk_ref[...] = g[128:256]
    gv_ref[...] = g[256:]


def attend_back(q, k, v, da, attn, stat, cos, sin, qm, km, pos, n1, wqkv):
    count, width = q.shape
    pairs = width // 128
    whole = lambda p: (0, 0)
    col = lambda p: (0, p)
    tall = pl.BlockSpec((count, 128), col)
    fixed = pl.BlockSpec((count, 128), whole)
    w = [pl.BlockSpec((128, width), lambda p, j=j: (p + j * pairs, 0)) for j in range(3)]
    grad = pl.BlockSpec((128, width), lambda p: (p, 0))
    small = pl.BlockSpec((8, 128), col)
    return pl.pallas_call(
        back_kernel,
        grid=(pairs,),
        in_specs=[tall] * 8 + [fixed] * 2 + [pl.BlockSpec((count, 2), whole), pl.BlockSpec((count, width), whole)] + w,
        out_specs=[grad] * 3 + [small] * 2 + [pl.BlockSpec((count, width), whole)],
        out_shape=[jax.ShapeDtypeStruct((width, width), BF16)] * 3
        + [jax.ShapeDtypeStruct((8, width), F32)] * 2
        + [jax.ShapeDtypeStruct((count, width), F32)],
        compiler_params=pltpu.CompilerParams(vmem_limit_bytes=56 * 2**20),
        name="attend_back",
    )(q, k, v, da, attn, stat, cos, sin, qm, km, pos, n1, wqkv, wqkv, wqkv)


from jax.sharding import PartitionSpec as P

HEADS = 12
STEP = 7


def place_tokens(heights, widths, count):
    sizes = heights * widths
    ends = jnp.cumsum(sizes)
    starts = ends - sizes
    places = jnp.arange(count, dtype=jnp.int32)
    segment = jnp.sum((places[:, None] >= ends[None, :]).astype(jnp.int32), axis=1)
    slots = jnp.arange(heights.shape[0], dtype=jnp.int32)
    picks = (segment[:, None] == slots[None, :]).astype(jnp.int32)
    begin = jnp.sum(picks * starts[None, :], axis=1)
    across = jnp.maximum(jnp.sum(picks * widths[None, :], axis=1), 1)
    offset = places - begin
    live = places < ends[-1]
    return (segment, offset // across, offset % across, live)


def layer_norm(value, gain, shift):
    centre = value - jnp.mean(value, axis=-1, keepdims=True)
    spread = jnp.mean(centre * centre, axis=-1, keepdims=True)
    return centre * lax.rsqrt(spread + 1e-06) * gain + shift


def adam(weight, first, second, grad, rate, decay):
    first_new = 0.5 * first + 0.5 * grad
    second_new = 0.5 * second + 0.5 * grad * grad
    correct = 1.0 - 0.5**STEP
    direction = first_new / correct / (jnp.sqrt(second_new / correct) + 1e-08)
    return (second_new, weight - rate * (direction + decay * weight))


def pairwise(bits, total):
    return [(i, i ^ bits) for i in range(total)]


def sum_everywhere(value, devices):
    if devices & (devices - 1):
        return lax.psum(value, "dp")
    step = 1
    while step < devices:
        value = value + lax.ppermute(value, "dp", pairwise(step, devices))
        step *= 2
    return value


def gather_weights(master, owner_block, devices):
    block_rows, width = master.shape
    low = master.astype(BF16)
    inverse = jnp.argsort(owner_block)
    if block_rows % 32:
        gathered = lax.all_gather(low, "dp", axis=0, tiled=True)
        return gathered.reshape(devices, block_rows, width)[inverse].reshape(-1, width)
    half = block_rows // 2
    core = lax.axis_index("group")
    mine = lax.all_gather(
        lax.dynamic_slice_in_dim(low, core * half, half, 0), "dp", axis=0, tiled=False
    )
    other = lax.ppermute(mine, "group", [(0, 1), (1, 0)])
    both = jnp.concatenate([mine, other], axis=0)
    first = inverse + devices * core
    second = inverse + devices * (1 - core)
    order = jnp.stack([first, second], axis=1).reshape(-1)
    return both[order].reshape(-1, width)


def reduce_grads(local_mat, owner_block, devices):
    rows, width = local_mat.shape
    block_rows = rows // devices
    if block_rows % 32 or devices != 16:
        term = local_mat.reshape(devices, block_rows, width)[owner_block].reshape(rows, width)
        share = lax.psum_scatter(term.astype(F32), "dp", scatter_dimension=0, tiled=True)
        return lax.psum(share.astype(BF16), "group").astype(F32)
    half = block_rows // 2
    core = lax.axis_index("group")
    me = lax.axis_index("dp")
    deep = me // 4
    flip = jnp.arange(2)

    def order(side):
        first = jnp.where(side == 0, 1, 2)
        second = 3 - first
        low_bits = (
            (me % 4)
            ^ (first * (1 - flip))[:, None, None]
            ^ (second * (1 - flip))[None, :, None]
        )
        dest = low_bits + 4 * jnp.arange(4)[None, None, :]
        return owner_block[dest.reshape(-1)] * 2 + side

    units = local_mat.reshape(2 * devices, half, width)
    give = units[order(1 - core)]
    keep = units[order(core)]
    got = lax.ppermute(give, "group", [(0, 1), (1, 0)])

    def add(one, two):
        return one.astype(F32) + two.astype(F32)

    def cross(bit0, bit1):
        total = 2 * devices
        perm = [(i, i ^ (bit0 if i < devices else bit1)) for i in range(total)]
        return lambda value: lax.ppermute(value, ("group", "dp"), perm)

    send = add(keep[:8], got[:8]).astype(BF16)
    hold = add(keep[8:], got[8:])
    came = cross(1, 2)(send)
    send = add(hold[:4], came[:4]).astype(BF16)
    hold = add(hold[4:], came[4:])
    came = cross(2, 1)(send)
    hold = add(hold, came)
    low = hold.astype(BF16)
    total = lax.dynamic_index_in_dim(hold, deep, 0, keepdims=False)
    for step in (1, 2, 3):
        part = lax.dynamic_index_in_dim(low, (deep + step) % 4, 0, keepdims=False)
        perm = [(i, (i + 4 * step) % 16) for i in range(16)]
        total = total + lax.ppermute(part, "dp", perm).astype(F32)
    other = lax.ppermute(total.astype(BF16), "group", [(0, 1), (1, 0)]).astype(F32)
    total = total.astype(BF16).astype(F32)
    top = jnp.where(core == 0, total, other)
    bottom = jnp.where(core == 0, other, total)
    return jnp.concatenate([top, bottom], axis=0)


def local(
    tokens,
    cotangent,
    grid_h,
    grid_w,
    owner_block,
    master,
    first_mom,
    second_mom,
    vectors,
    vec_first,
    vec_second,
):
    devices = lax.axis_size("dp")
    count = tokens.shape[1]
    width = tokens.shape[2]
    heads = HEADS
    head_dim = width // heads
    half = head_dim // 2
    segment, rows_pos, cols_pos, live = place_tokens(grid_h[0], grid_w[0], count)
    weights = gather_weights(master, owner_block, devices)
    w_qkv = weights[: 3 * width]
    w_proj = weights[3 * width : 4 * width]
    w_up = weights[4 * width : 8 * width]
    w_down = weights[8 * width :]

    freqs = vectors[13]

    def spread(part):
        return jnp.broadcast_to(part.reshape(heads, 1, half), (heads, 2, half)).reshape(1, width)

    angle = rows_pos.astype(F32)[:, None] * spread(freqs[: width // 2]) + cols_pos.astype(F32)[
        :, None
    ] * spread(freqs[width // 2 :])
    lower = (jnp.arange(width) % head_dim < half)[None]
    cosine = jnp.cos(angle)
    sine = jnp.sin(angle)
    sine = jnp.where(lower, -sine, sine)
    ids = jnp.arange(128)[None]
    match = segment[:, None] == ids
    key_mask = jnp.where(match | ((ids >= 8) & (ids < 11)), 1.0, 0.0).astype(BF16)
    query_mask = jnp.where((ids < 8) & ~match, MASKED, 0.0).astype(BF16)
    places = jnp.stack([rows_pos, cols_pos], axis=1).astype(F32)

    first_in, query, key, value, attn_out, stat = attend(
        tokens[0], vectors[0:1], vectors[1:2], w_qkv, vectors[4:7].reshape(1, 3 * width),
        cosine, sine, query_mask, key_mask,
    )
    inputs = tokens[0].astype(F32)
    middle = inputs + mm(attn_out, w_proj, LAST) + vectors[7]
    normed_second, norm_two_back = jax.vjp(layer_norm, middle, vectors[2], vectors[3])
    second_in = normed_second.astype(BF16)
    grad_two = jnp.where(live[:, None], cotangent[0], jnp.zeros((), BF16))
    grad_out = grad_two.astype(F32)
    branch_two, grad_second_in, grad_up, grad_down, bias_up = mlp(
        second_in, grad_two, w_up, w_down, vectors[8:12].reshape(1, 4 * width)
    )
    block_out = (middle + branch_two + vectors[12]).astype(BF16)
    bias_down = jnp.sum(grad_out, axis=0)
    grad_mid_norm, gain_two, shift_two = norm_two_back(grad_second_in)
    grad_middle = grad_out + grad_mid_norm
    grad_one = grad_middle.astype(BF16)
    grad_proj = mm(grad_one, attn_out, FIRST).astype(BF16)
    bias_proj = jnp.sum(grad_one.astype(F32), axis=0)
    grad_attn = mm(grad_one, w_proj, PLAIN).astype(BF16)
    grad_q, grad_k, grad_v, grad_bias, grad_freq, grad_first_in = attend_back(
        query, key, value, grad_attn, attn_out, stat, cosine, sine, query_mask, key_mask,
        places, first_in, w_qkv,
    )
    unused, norm_one_back = jax.vjp(layer_norm, inputs, vectors[0], vectors[1])
    grad_in_norm, gain_one, shift_one = norm_one_back(grad_first_in)
    input_grad = grad_middle + grad_in_norm
    grad_freqs = grad_freq[:2].reshape(2, heads, 2, half).sum(2).reshape(1, width)
    local_vec = jnp.concatenate(
        [
            gain_one[None],
            shift_one[None],
            gain_two[None],
            shift_two[None],
            grad_bias[:3],
            bias_proj[None],
            bias_up.reshape(4, width),
            bias_down[None],
            grad_freqs,
        ],
        axis=0,
    )
    local_mat = jnp.concatenate([grad_q, grad_k, grad_v, grad_proj, grad_up, grad_down], axis=0)
    share = reduce_grads(local_mat, owner_block, devices)
    vec_total = sum_everywhere(lax.psum(local_vec, "group") if devices & (devices - 1) else
                               local_vec + lax.ppermute(local_vec, "group", [(0, 1), (1, 0)]), devices)
    square = sum_everywhere(jnp.sum(share * share).reshape(1, 1), devices)[0, 0]
    grad_norm = jnp.sqrt(square + jnp.sum(vec_total * vec_total))
    clip = jnp.minimum(1.0, 1.0 / (grad_norm + 1e-06))
    mat_grad = share * clip
    vec_grad = vec_total * clip
    mat_second, mat_weight = adam(master, first_mom, second_mom, mat_grad, 0.02, 0.05)
    vec_second_new, vec_weight = adam(vectors, vec_first, vec_second, vec_grad, 0.2, 0.0)
    return (
        block_out[None],
        input_grad[None],
        mat_grad,
        mat_second,
        mat_weight,
        vec_grad,
        vec_second_new,
        vec_weight,
        grad_norm,
    )


def solution(mesh):
    return jax.shard_map(
        local,
        mesh=mesh,
        in_specs=(
            P("group", "dp", None),
            P("group", "dp", None),
            P("group", "dp"),
            P("group", "dp"),
            P(),
            P("dp", None),
            P("dp", None),
            P("dp", None),
            P(),
            P(),
            P(),
        ),
        out_specs=(
            P("group", "dp", None),
            P("group", "dp", None),
            P("dp", None),
            P("dp", None),
            P("dp", None),
            P(),
            P(),
            P(),
            P(),
        ),
        check_vma=False,
    )
```

time: 1220 us -> 536 us (0.44)
  waiting for transfers between devices: 496 us -> 194 us
  matrix products: 288 us -> 8.55 us
  Pallas kernels: 0 us -> 139 us
  other arithmetic: 162 us -> 73.2 us
  blocking collectives: 86.4 us -> 0 us
  local copies, waits for them, and re-layouts: 153 us -> 69.9 us
  starting transfers between devices: 0.12 us -> 27.4 us
    reduce_scatter x1 -> x0, waiting for transfers between devices: 326 us -> none  [local(): share = lax.psum_scatter(owner_term, 'dp', scatter_dimension=0, tiled=True)]
    dot_general x26 -> x3, matrix products: 288 us -> 8.55 us  [mm(): return lax.dot_general(left, right, dims, preferred_element_type=F32)]
    pallas_call x0 -> x3, Pallas kernels: none -> 139 us  [the longest x1 56.4 us: mlp(): pl.pallas_call(mlp_kernel, grid=(units // tile,), in_specs=[pl.BlockSpec(...]
    ppermute x0 -> x17, waiting for transfers between devices: none -> 87.8 us  [the longest x2 57.9 us: cross(): return lambda value: lax.ppermute(value, ('group', 'dp'), perm)]
    psum x2 -> x0, blocking collectives: 86.4 us -> none  [the longest x1 43.8 us: local(): vec_total = lax.psum(local_vec, ('group', 'dp'))]
    dynamic_update_slice x4 -> x0, local copies, waits for them, and re-layouts: 63.4 us -> none  [local(): lax.scan(back_step, (zero_heads, zero_heads), jnp.arange(block_count))]
    all_gather x1, waiting for transfers between devices: 161 us -> 106 us  [gather_weights(): lax.all_gather(lax.dynamic_slice_in_dim(low, core * half, half, 0), 'dp',...]
    reduce_sum x6 -> x4, other arithmetic: 34.2 us -> 3.22 us  [the longest x1 1.59 us: local(): bias_down = jnp.sum(grad_out, axis=0)]
  transfers between devices with their start and end apart: 3 -> 18, of which waited for: 3 -> 13; matrix products, arithmetic and copies ran while one was open for 4% -> 10% of each run, Pallas kernels for 0% -> 0%
where the time goes in v1:
time: 536 us; the launch traced here: 532 us
  waiting for transfers between devices  194 us (36%)
  Pallas kernels  139 us (26%)
  other arithmetic  73.2 us (14%)
  local copies, waits for them, and re-layouts  69.9 us (13%)
  starting transfers between devices  27.4 us (5%)
  between operations  20.1 us (4%)
  matrix products  8.55 us (2%)
    all_gather x1, waiting for transfers between devices, gather_weights(): lax.all_gather(lax.dynamic_slice_in_dim(low, core * half, half, 0), 'dp',...  106 us
    ppermute x2, waiting for transfers between devices, cross(): return lambda value: lax.ppermute(value, ('group', 'dp'), perm)  57.9 us
    pallas_call x1, Pallas kernels, mlp(): pl.pallas_call(mlp_kernel, grid=(units // tile,), in_specs=[pl.BlockSpec(...  56.4 us
    pallas_call x1, Pallas kernels, attend_back(): pl.pallas_call(back_kernel, grid=(pairs,), in_specs=[tall] * 8 + [fixed]...  53.1 us
    pallas_call x1, Pallas kernels, attend(): pl.pallas_call(attend_kernel, grid=(pairs,), in_specs=specs, out_specs=ou...  29.3 us
    ppermute x8, waiting for transfers between devices, sum_everywhere(): value = value + lax.ppermute(value, 'dp', pairwise(step, devices))  26.9 us
    ppermute x8, starting transfers between devices, sum_everywhere(): value = value + lax.ppermute(value, 'dp', pairwise(step, devices))  19.3 us
    unnamed x62, local copies, waits for them, and re-layouts  16.2 us
  transfers between devices with their start and end apart: 18, of which 13 were waited for; matrix products, arithmetic and copies ran while one was open for 10% of the time, Pallas kernels for 0%

profile of v1, /device:TPU:0, one launch (start us, length us, event | category | flops | bytes accessed | tf_op | source)
XLA Modules:
  0.0 531.9 jit_solution(7153660905851242959)
XLA Ops:
  9.3 106.1 %all-gather.3.cloned.1.call-done = bf16[4608,768]{1,0:T(8,128)(2,1)} async-done(((bf16[288,768]{1,0:T(8,128)(2,1)}), bf16[4608,768]{1,0:T(8,128)(2,1)}) %all-gather.3.cloned.1.call-update) | async-done | bytes 7077904 | tf_op jit(solution)/shard_map/all_gather | solution.py:357
  132.2 13.5 %negate_select_fusion = (f32[1024,768]{1,0:T(8,128)}, f32[1024,768]{1,0:T(8,128)}) fusion(f32[768]{0:T(1024)S(1)} %mul.334, f32[1024]{0:T(1024)S(1)} %get-tuple-element.95, f32[768]{0:T(1024)S(1)} %mul.330, f32[1024]{0:T(1024)S(1)} %get-tuple-element.94, pred[768]{0:T(1024)(128)(4,1)S(1)} %fusion.38), kind=kLoop, calls=%fused_computation.10 | loop fusion | flops 3932160 | bytes 6306560 | tf_op jit(solution)/shard_map/jit(_where)/select_n | solution.py:462
  145.7 10.0 %pad_maximum_fusion = bf16[32,288,768]{2,1,0:T(8,128)(2,1)} fusion(bf16[16,288,768]{2,1,0:T(8,128)(2,1)} %collective-permute-done, bf16[16,288,768]{2,1,0:T(8,128)(2,1)S(1)} %bitcast.93), kind=kLoop, calls=%fused_computation.5 | loop fusion | flops 7077888 | bytes 28311552 | tf_op jit(solution)/shard_map/concatenate | solution.py:361
  155.7 12.4 %gather_fusion = bf16[32,288,768]{2,1,0:T(8,128)(2,1)} fusion(bf16[32,288,768]{2,1,0:T(8,128)(2,1)} %pad_maximum_fusion, s32[1024]{0:T(1024)S(1)} %pad_clamp_fusion.4), kind=kCustom, calls=%fused_computation | custom fusion | bytes 28311680 | tf_op jit(solution)/shard_map/gather | solution.py:365
  168.1 4.0 slice.121
  172.1 8.0 %fusion.62 = (bf16[3072,768]{1,0:T(8,128)(2,1)}, bf16[3072,768]{1,0:T(8,128)(2,1)}) fusion(bf16[9216,768]{1,0:T(8,128)(2,1)} %bitcast.86), kind=kLoop, calls=%fused_computation.170 | loop fusion | bytes 18874368 | tf_op jit(solution)/shard_map/slice | solution.py:449
  180.1 29.3 %attend.1 = (bf16[1024,768]{1,0:T(8,128)(2,1)}, bf16[1024,768]{1,0:T(8,128)(2,1)}, bf16[1024,768]{1,0:T(8,128)(2,1)}, bf16[1024,768]{1,0:T(8,128)(2,1)}, bf16[1024,768]{1,0:T(8,128)(2,1)}, /*index=5*/f32[1024,768]{1,0:T(8,128)}) custom-call(bf16[1024,768]{1,0:T(8,128)(2,1)} %bitcast.89, f32[1,768]{1,0:T(1,128)} %get-tuple-element.89.g_ref, ...), custom_call_target="tpu_custom_call" | custom-call | tf_op jit(solution)/shard_map/attend/pallas_call | solution.py:119
  209.4 3.3 fusion.63
  214.9 56.4 %mlp.1 = (f32[1024,768]{1,0:T(8,128)}, f32[1024,768]{1,0:T(8,128)}, bf16[3072,768]{1,0:T(8,128)(2,1)}, bf16[3072,768]{1,0:T(8,128)(2,1)}, f32[1,3072]{1,0:T(1,128)}) custom-call(bf16[1024,768]{1,0:T(8,128)(2,1)} %add_convert_fusion.2.n2_ref, bf16[1024,768]{1,0:T(8,128)(2,1)} %get-tuple-element.71.dz_ref, bf16[3072,768]{1,0:T(8,128)(2,1)} %get-tuple-element.81.w1_ref, ...), custom_call_target="tpu_custom_call" | custom-call | tf_op jit(solution)/shard_map/mlp/pallas_call | solution.py:176
  271.4 3.0 multiply_reduce_fusion
  279.2 3.8 convolution_convert_fusion.da_ref
  283.0 53.1 %attend_back.1 = (bf16[768,768]{1,0:T(8,128)(2,1)}, bf16[768,768]{1,0:T(8,128)(2,1)}, bf16[768,768]{1,0:T(8,128)(2,1)}, f32[8,768]{1,0:T(8,128)}, f32[8,768]{1,0:T(8,128)}, /*index=5*/f32[1024,768]{1,0:T(8,128)}) custom-call(bf16[1024,768]{1,0:T(8,128)(2,1)} %get-tuple-element.31.q_ref, bf16[1024,768]{1,0:T(8,128)(2,1)} %get-tuple-element.32.k_ref, ...), custom_call_target="tpu_custom_call" | custom-call | tf_op jit(solution)/shard_map/attend_back/pallas_call | solution.py:286
  342.7 5.0 copy-done.6
  347.8 8.8 %gather_fusion.4 = bf16[16,288,768]{2,1,0:T(8,128)(2,1)} fusion(bf16[32,288,768]{2,1,0:T(8,128)(2,1)} %bitcast.90, s32[1024]{0:T(1024)S(1)} %pad_clamp_fusion), kind=kCustom, calls=%fused_computation.4 | custom fusion | bytes 14155840 | tf_op jit(solution)/shard_map/gather | solution.py:393
  357.8 8.9 %gather_fusion.2 = bf16[16,288,768]{2,1,0:T(8,128)(2,1)} fusion(bf16[32,288,768]{2,1,0:T(8,128)(2,1)} %bitcast.91, s32[1024]{0:T(1024)S(1)} %pad_clamp_fusion.2), kind=kCustom, calls=%fused_computation.2 | custom fusion | bytes 14155840 | tf_op jit(solution)/shard_map/gather | solution.py:394
  368.4 6.1 %add_convert_fusion = (bf16[8,288,768]{2,1,0:T(8,128)(2,1)S(1)}, f32[8,288,768]{2,1,0:T(8,128)S(1)}) fusion(bf16[16,288,768]{2,1,0:T(8,128)(2,1)} %collective-permute-done.1, bf16[16,288,768]{2,1,0:T(8,128)(2,1)} %gather_fusion.2), kind=kLoop, calls=%fused_computation.6 | loop fusion | flops 12386304 | bytes 24772608 | tf_op jit(solution)/shard_map/convert_element_type | solution.py:405
  376.0 40.0 %collective-permute-done.2 = bf16[8,288,768]{2,1,0:T(8,128)(2,1)S(1)} collective-permute-done((bf16[8,288,768]{2,1,0:T(8,128)(2,1)S(1)}, bf16[8,288,768]{2,1,0:T(8,128)(2,1)S(1)}, u32[]{:S(2)}, u32[]{:S(2)}) %collective-permute-start.2) | collective-permute-done | bytes 3538976 | tf_op jit(solution)/shard_map/ppermute | solution.py:403
  421.4 3.2 fusion.54
  424.6 17.9 %collective-permute-done.3 = bf16[4,288,768]{2,1,0:T(8,128)(2,1)} collective-permute-done((bf16[4,288,768]{2,1,0:T(8,128)(2,1)}, bf16[4,288,768]{2,1,0:T(8,128)(2,1)}, u32[]{:S(2)}, u32[]{:S(2)}) %collective-permute-start.3) | collective-permute-done | bytes 1769504 | tf_op jit(solution)/shard_map/ppermute | solution.py:403
  442.5 5.2 fusion.59
  466.9 14.0 %collective-permute-done.15 = f32[14,768]{1,0:T(8,128)S(1)} collective-permute-done((f32[14,768]{1,0:T(8,128)S(1)}, f32[14,768]{1,0:T(8,128)S(1)}, u32[]{:S(2)}, u32[]{:S(2)}) %collective-permute-start.15) | collective-permute-done | bytes 43040 | tf_op jit(solution)/shard_map/ppermute | solution.py:343
  484.1 4.7 add_bitcast_fusion
  503.1 8.1 %collective-permute-start.10 = (f32[1,1]{1,0:T(1,128)}, f32[1,1]{1,0:T(1,128)}, u32[]{:S(2)}, u32[]{:S(2)}) collective-permute-start(f32[1,1]{1,0:T(1,128)} %add.438), channel_id=1, source_target_pairs={{0,4},{1,5},{2,6},{3,7},{4,0},{5,1},{6,2},{7,3},{8,12},{9,13},{10,... | collective-permute-start | bytes 20 | tf_op jit(solution)/shard_map/ppermute | solution.py:343
  518.0 4.9 fusion.18
  (187 shorter events, 82.0 us)
Async XLA Ops:
  7.2 123.5 %copy-start.13 = (bf16[1,1024,768]{2,1,0:T(8,128)(2,1)S(1)}, bf16[1,1024,768]{2,1,0:T(8,128)(2,1)}, u32[]{:S(2)}) copy-start(bf16[1,1024,768]{2,1,0:T(8,128)(2,1)} %param.12) | copy-start | bytes 4718596
  7.2 108.3 %all-gather.3.cloned.1.call-start = ((), (), s32[]{:S(2)}) async-start(), calls=%async_computation | async-start | bytes 7520256 | tf_op jit(solution)/shard_map/all_gather | solution.py:357
  115.4 30.3 %collective-permute-start = (bf16[16,288,768]{2,1,0:T(8,128)(2,1)}, bf16[16,288,768]{2,1,0:T(8,128)(2,1)}, u32[]{:S(2)}, u32[]{:S(2)}) collective-permute-start(bf16[16,288,768]{2,1,0:T(8,128)(2,1)} %bitcast.92), channel_id=1, source_target_pairs={{0,16},{16,0},{1,17},{17,1},{2,18},{18,2},{3,19},{19,3},{4,20},{20... | collective-permute-start | bytes 21233672 | tf_op jit(solution)/shard_map/ppermute | solution.py:360
  130.6 15.1 %copy-start.8 = (bf16[4608,768]{1,0:T(8,128)(2,1)S(1)}, bf16[4608,768]{1,0:T(8,128)(2,1)}, u32[]{:S(2)}) copy-start(bf16[4608,768]{1,0:T(8,128)(2,1)} %all-gather.3.cloned.1.call-done) | copy-start | bytes 21233668
  180.1 29.3 %copy-start.1 = (bf16[1,1024,768]{2,1,0:T(8,128)(2,1)S(1)}, bf16[1,1024,768]{2,1,0:T(8,128)(2,1)}, u32[]{:S(2)}) copy-start(bf16[1,1024,768]{2,1,0:T(8,128)(2,1)} %param.11) | copy-start | bytes 4718596
  356.6 11.8 %collective-permute-start.1 = (bf16[16,288,768]{2,1,0:T(8,128)(2,1)}, bf16[16,288,768]{2,1,0:T(8,128)(2,1)}, u32[]{:S(2)}, u32[]{:S(2)}) collective-permute-start(bf16[16,288,768]{2,1,0:T(8,128)(2,1)} %gather_fusion.4), channel_id=1, source_target_pairs={{0,16},{16,0},{1,17},{17,1},{2,18},{18,2},{3,19},{19,3},{4,20},{20... | collective-permute-start | bytes 21233672 | tf_op jit(solution)/shard_map/ppermute | solution.py:395
  374.5 45.1 %copy-start.2 = (f32[8,288,768]{2,1,0:T(8,128)}, f32[8,288,768]{2,1,0:T(8,128)S(1)}, u32[]{:S(2)}) copy-start(f32[8,288,768]{2,1,0:T(8,128)S(1)} %get-tuple-element.79) | copy-start | bytes 21233668
  374.5 41.5 %collective-permute-start.2 = (bf16[8,288,768]{2,1,0:T(8,128)(2,1)S(1)}, bf16[8,288,768]{2,1,0:T(8,128)(2,1)S(1)}, u32[]{:S(2)}, u32[]{:S(2)}) collective-permute-start(bf16[8,288,768]{2,1,0:T(8,128)(2,1)S(1)} %get-tuple-element.78), channel_id=1, source_target_pairs={{0,1},{1,0},{2,3},{3,2},{4,5},{5,4},{6,7},{7,6},{8,9},{9,8},{10,11... | collective-permute-start | bytes 10616840 | tf_op jit(solution)/shard_map/ppermute | solution.py:403
  419.6 22.8 %collective-permute-start.3 = (bf16[4,288,768]{2,1,0:T(8,128)(2,1)}, bf16[4,288,768]{2,1,0:T(8,128)(2,1)}, u32[]{:S(2)}, u32[]{:S(2)}) collective-permute-start(bf16[4,288,768]{2,1,0:T(8,128)(2,1)} %fusion.4), channel_id=1, source_target_pairs={{0,2},{1,3},{2,0},{3,1},{4,6},{5,7},{6,4},{7,5},{8,10},{9,11},{10,... | collective-permute-start | bytes 5308424 | tf_op jit(solution)/shard_map/ppermute | solution.py:403
  421.1 21.4 %copy-start.10 = (bf16[8,288,768]{2,1,0:T(8,128)(2,1)S(1)}, bf16[8,288,768]{2,1,0:T(8,128)(2,1)}, u32[]{:S(2)}) copy-start(bf16[8,288,768]{2,1,0:T(8,128)(2,1)} %copy-done.9) | copy-start | bytes 10616836
  448.8 33.5 %collective-permute-start.4 = (bf16[288,768]{1,0:T(8,128)(2,1)}, bf16[288,768]{1,0:T(8,128)(2,1)}, u32[]{:S(2)}, u32[]{:S(2)}) collective-permute-start(bf16[288,768]{1,0:T(8,128)(2,1)} %get-tuple-element.83), channel_id=1, source_target_pairs={{0,4},{1,5},{2,6},{3,7},{4,8},{5,9},{6,10},{7,11},{8,12},{9,13},{1... | collective-permute-start | bytes 1327112 | tf_op jit(solution)/shard_map/ppermute | solution.py:417
  449.3 33.0 %collective-permute-start.5 = (bf16[288,768]{1,0:T(8,128)(2,1)}, bf16[288,768]{1,0:T(8,128)(2,1)}, u32[]{:S(2)}, u32[]{:S(2)}) collective-permute-start(bf16[288,768]{1,0:T(8,128)(2,1)} %get-tuple-element.85), channel_id=1, source_target_pairs={{0,8},{1,9},{2,10},{3,11},{4,12},{5,13},{6,14},{7,15},{8,0},{9,1},... | collective-permute-start | bytes 1327112 | tf_op jit(solution)/shard_map/ppermute | solution.py:417
  450.8 31.5 %collective-permute-start.6 = (bf16[288,768]{1,0:T(8,128)(2,1)}, bf16[288,768]{1,0:T(8,128)(2,1)}, u32[]{:S(2)}, u32[]{:S(2)}) collective-permute-start(bf16[288,768]{1,0:T(8,128)(2,1)} %get-tuple-element.84), channel_id=1, source_target_pairs={{0,12},{1,13},{2,14},{3,15},{4,0},{5,1},{6,2},{7,3},{8,4},{9,5},{1... | collective-permute-start | bytes 1327112 | tf_op jit(solution)/shard_map/ppermute | solution.py:417
  457.2 1.3 collective-permute-start.12
  458.5 4.2 collective-permute-start.13
  462.7 4.2 collective-permute-start.14
  466.8 14.1 %collective-permute-start.15 = (f32[14,768]{1,0:T(8,128)S(1)}, f32[14,768]{1,0:T(8,128)S(1)}, u32[]{:S(2)}, u32[]{:S(2)}) collective-permute-start(f32[14,768]{1,0:T(8,128)S(1)} %add.443), channel_id=1, source_target_pairs={{0,4},{1,5},{2,6},{3,7},{4,0},{5,1},{6,2},{7,3},{8,12},{9,13},{10,... | collective-permute-start | bytes 129032 | tf_op jit(solution)/shard_map/ppermute | solution.py:343
  480.9 10.6 %collective-permute-start.16 = (f32[14,768]{1,0:T(8,128)S(1)}, f32[14,768]{1,0:T(8,128)S(1)}, u32[]{:S(2)}, u32[]{:S(2)}) collective-permute-start(f32[14,768]{1,0:T(8,128)S(1)} %add.444), channel_id=1, source_target_pairs={{0,8},{1,9},{2,10},{3,11},{4,12},{5,13},{6,14},{7,15},{8,0},{9,1},... | collective-permute-start | bytes 129032 | tf_op jit(solution)/shard_map/ppermute | solution.py:343
  484.0 8.7 %collective-permute-start.7 = (bf16[288,768]{1,0:T(8,128)(2,1)S(1)}, bf16[288,768]{1,0:T(8,128)(2,1)S(1)}, u32[]{:S(2)}, u32[]{:S(2)}) collective-permute-start(bf16[288,768]{1,0:T(8,128)(2,1)S(1)} %fusion.26), channel_id=1, source_target_pairs={{0,16},{16,0},{1,17},{17,1},{2,18},{18,2},{3,19},{19,3},{4,20},{20... | collective-permute-start | bytes 1327112 | tf_op jit(solution)/shard_map/ppermute | solution.py:418
  488.9 29.1 %copy-start.12 = (f32[576,768]{1,0:T(8,128)S(1)}, f32[576,768]{1,0:T(8,128)}, u32[]{:S(2)}) copy-start(f32[576,768]{1,0:T(8,128)} %param.16) | copy-start | bytes 5308420
  493.9 3.6 collective-permute-start.8
  498.9 3.6 collective-permute-start.9
  503.1 8.3 %collective-permute-start.10 = (f32[1,1]{1,0:T(1,128)}, f32[1,1]{1,0:T(1,128)}, u32[]{:S(2)}, u32[]{:S(2)}) collective-permute-start(f32[1,1]{1,0:T(1,128)} %add.438), channel_id=1, source_target_pairs={{0,4},{1,5},{2,6},{3,7},{4,0},{5,1},{6,2},{7,3},{8,12},{9,13},{10,... | collective-permute-start | bytes 20 | tf_op jit(solution)/shard_map/ppermute | solution.py:343
  512.1 4.5 collective-permute-start.11
  (21 other events, 89.0 us)
Sparse Core Ops, SparseCore 0:
  11.4 104.0 all-gather.2

commit v2 on v1

v2 whole, which is shorter than its diff:
```python
import functools
import jax
import jax.numpy as jnp
from jax import lax
from jax.experimental import pallas as pl
from jax.experimental.pallas import tpu as pltpu

F32 = jnp.float32
BF16 = jnp.bfloat16
LAST = (((1,), (1,)), ((), ()))
FIRST = (((0,), (0,)), ((), ()))
PLAIN = (((1,), (0,)), ((), ()))
MASKED = -1e9


def mm(left, right, dims):
    return lax.dot_general(left, right, dims, preferred_element_type=F32)


def norm_parts(value):
    centre = value - jnp.mean(value, axis=-1, keepdims=True)
    spread = jnp.mean(centre * centre, axis=-1, keepdims=True)
    inverse = lax.rsqrt(spread + 1e-6)
    return centre * inverse, inverse


def norm_back(unit, inverse, grad, gain):
    scaled = grad * gain
    first = jnp.mean(scaled, axis=-1, keepdims=True)
    second = jnp.mean(scaled * unit, axis=-1, keepdims=True)
    return inverse * (scaled - first - unit * second)


def swap_halves(value):
    lane = lax.broadcasted_iota(jnp.int32, value.shape, 1)
    return jnp.where(
        lane % 64 < 32, pltpu.roll(value, 96, 1), pltpu.roll(value, 32, 1)
    )


def split3(value):
    one = value.astype(BF16).astype(F32)
    rest = value - one
    two = rest.astype(BF16).astype(F32)
    return one, two, rest - two


LARGE = 208
SMALL = 80


def place_pieces(core, slot_ref, mine, other, block, side, dst, sem):
    for which, (first, second, small) in enumerate((mine, other)):
        @pl.when((core == side) if which == 0 else (core != side))
        def _():
            large_slot = slot_ref[2 * which, block]
            small_slot = slot_ref[2 * which + 1, block]

            @pl.when(large_slot < 8)
            def _():
                pltpu.make_async_copy(first.at[large_slot], dst(0, LARGE), sem).start()

            @pl.when(large_slot >= 8)
            def _():
                pltpu.make_async_copy(second.at[large_slot - 8], dst(0, LARGE), sem).start()

            pltpu.make_async_copy(small.at[small_slot], dst(LARGE, SMALL), sem).start()


def attend_kernel(blocks, core_ref, slot_ref, x_ref, g_ref, b_ref, bq_ref, bk_ref, bv_ref,
                  cos_ref, sin_ref, qm_ref, km_ref, *rest):
    if blocks:
        mine, other = rest[0:3], rest[3:6]
        n1_ref, q_ref, k_ref, v_ref, attn_ref, stat_ref, w_ref, n1_s, w_s, near, far = rest[6:]
    else:
        w_ref, n1_ref, q_ref, k_ref, v_ref, attn_ref, stat_ref, n1_s, w_s, near = rest
    count, width = x_ref.shape
    step = pl.program_id(0)

    @pl.when(step == 0)
    def _():
        if blocks:
            core = core_ref[0]
            rows = w_ref.shape[0] // blocks

            def start(block, target, sem):
                for side in (0, 1):
                    def dst(offset, size):
                        base = block * rows + side * (rows // 2) + offset
                        return target.at[pl.ds(pl.multiple_of(base, 16), size)]
                    place_pieces(core, slot_ref, mine, other, block, side, dst, sem)

            def near_block(block, carry):
                start(block, w_s, near)
                return carry

            def far_block(block, carry):
                start(block, w_ref, far)
                return carry

            lax.fori_loop(0, w_s.shape[0] // rows, near_block, 0)
            lax.fori_loop(0, blocks, far_block, 0)
        else:
            pltpu.make_async_copy(w_ref.at[pl.ds(0, 3 * width)], w_s, near).start()
        unit, _ = norm_parts(x_ref[...].astype(F32))
        n1 = (unit * g_ref[...] + b_ref[...]).astype(BF16)
        n1_s[...] = n1
        n1_ref[...] = n1
        pltpu.make_async_copy(w_s, w_s, near).wait()

    def third(j):
        return w_s[pl.ds(pl.multiple_of(j * width + step * 128, 128), 128), :]

    w = jnp.concatenate([third(0), third(1), third(2)], axis=0)
    qkv = mm(n1_s[...], w, LAST)
    q = qkv[:, :128] + bq_ref[...]
    k = qkv[:, 128:256] + bk_ref[...]
    v = (qkv[:, 256:] + bv_ref[...]).astype(BF16)
    c = cos_ref[...]
    s = sin_ref[...]
    qr = ((q * c + swap_halves(q) * s).astype(BF16).astype(F32) * 0.125).astype(BF16)
    kr = (k * c + swap_halves(k) * s).astype(BF16)
    q_ref[...] = qr
    k_ref[...] = kr
    v_ref[...] = v
    lane = lax.broadcasted_iota(jnp.int32, (1, 128), 1)
    k_aug = jnp.concatenate([kr, km_ref[...]], axis=1)
    v_aug = jnp.concatenate([v, jnp.ones((count, 128), BF16)], axis=1)
    zero = jnp.zeros((), BF16)
    tile = 256
    for i in range(count // tile):
        rows = pl.ds(i * tile, tile)
        out = None
        stats = []
        for h in (0, 1):
            mine_lanes = (lane // 64) == h
            qa = jnp.concatenate(
                [jnp.where(mine_lanes, qr[i * tile:(i + 1) * tile], zero), qm_ref[rows, :]], axis=1)
            scores = mm(qa, k_aug, LAST)
            top = jnp.max(scores, axis=-1, keepdims=True)
            e = jnp.exp(scores - top).astype(BF16)
            o = mm(e, v_aug, PLAIN)
            total = o[:, 128:]
            o = o[:, :128] / total
            out = o if out is None else jnp.where(lane < 64, out, o)
            stats.append(top + jnp.log(total[:, :1]))
        attn_ref[rows, :] = out.astype(BF16)
        stat_ref[rows, :] = jnp.where(lane < 64, stats[0], stats[1])

    if blocks:
        @pl.when(step == pl.num_programs(0) - 1)
        def _():
            pltpu.make_async_copy(w_ref, w_ref, far).wait()


def attend(core, slots, x, gain, shift, bqkv, cos, sin, qm, km, weights, stack):
    count, width = x.shape
    pairs = width // 128
    pieces = isinstance(weights, tuple)
    blocks = slots.shape[1] if pieces else 0
    whole = lambda p: (0, 0)
    col = lambda p: (0, p)
    smem = pl.BlockSpec(memory_space=pltpu.SMEM)
    hbm = pl.BlockSpec(memory_space=pl.ANY)
    given = weights if pieces else (weights,)
    specs = [smem, smem] + [
        pl.BlockSpec((count, width), whole),
        pl.BlockSpec((1, width), whole),
        pl.BlockSpec((1, width), whole),
        pl.BlockSpec((1, 128), col),
        pl.BlockSpec((1, 128), lambda p: (0, p + pairs)),
        pl.BlockSpec((1, 128), lambda p: (0, p + 2 * pairs)),
        pl.BlockSpec((count, 128), col),
        pl.BlockSpec((count, 128), col),
        pl.BlockSpec((count, 128), whole),
        pl.BlockSpec((count, 128), whole),
    ] + [hbm] * len(given)
    outs = [pl.BlockSpec((count, width), whole)] + [pl.BlockSpec((count, 128), col)] * 5
    shape = lambda d: jax.ShapeDtypeStruct((count, width), d)
    shapes = [shape(BF16)] * 5 + [shape(F32)]
    scratch = [pltpu.VMEM((count, width), BF16), pltpu.VMEM((3 * width, width), BF16), pltpu.SemaphoreType.DMA]
    if pieces:
        outs.append(hbm)
        shapes.append(jax.ShapeDtypeStruct((stack, width), BF16))
        scratch.append(pltpu.SemaphoreType.DMA)
    return pl.pallas_call(
        functools.partial(attend_kernel, blocks),
        grid=(pairs,),
        in_specs=specs,
        out_specs=outs,
        out_shape=shapes,
        scratch_shapes=scratch,
        compiler_params=pltpu.CompilerParams(vmem_limit_bytes=56 * 2**20),
        cost_estimate=pl.CostEstimate(flops=30 * 10**9, bytes_accessed=40 * 10**6, transcendentals=0),
        name="attend",
    )(core, slots, x, gain, shift, bqkv, bqkv, bqkv, cos, sin, qm, km, *given)


HALF_ERFC = (
    0.09317889578353007, 0.09147806194869737, 0.10061136147272338, 0.023612303617162326,
    0.20424612730309272, -0.1755704972361086, 0.23011593265708702, -0.06767218931083122,
)


def gelu_both(x):
    e = jnp.exp(x * x * -0.5)
    d = jnp.abs(x) * (0.33 * 0.7071067811865476) + 1.0
    t = pl.reciprocal(d, approx=True)
    t = t * (2.0 - d * t)
    poly = jnp.full_like(t, HALF_ERFC[-1])
    for c in HALF_ERFC[-2::-1]:
        poly = poly * t + c
    tail = poly * t * e
    cdf = jnp.where(x >= 0, 1.0 - tail, tail)
    return x * cdf, cdf + x * e * 0.3989422804014327


def send_rows(core, block_rows, stage, row, base, keep_ref, give_ref, sem):
    if not block_rows:
        rows = stage.shape[0]
        pltpu.make_async_copy(
            stage, keep_ref.at[pl.ds(pl.multiple_of(row - base, 64), rows)], sem
        ).start()
        return

    def one(index, carry):
        at = row + 64 * index
        block = lax.div(at, block_rows)
        inner = pl.ds(pl.multiple_of(at - block * block_rows, 64), 64)
        slot = lax.div(block, 2) - base // 2
        source = stage.at[pl.ds(pl.multiple_of(64 * index, 64), 64)]
        own = lax.rem(block, 2) == core

        @pl.when(own)
        def _():
            pltpu.make_async_copy(source, keep_ref.at[slot, inner], sem).start()

        @pl.when(jnp.logical_not(own))
        def _():
            pltpu.make_async_copy(source, give_ref.at[slot, inner], sem).start()

        return carry

    lax.fori_loop(0, stage.shape[0] // 64, one, 0)


def mlp_kernel(block_rows, base, core_ref, x_ref, at_ref, cot_ref, live_ref, vec_ref, wo_ref, w1_ref, w2_ref, b1_ref,
               out_ref, dm_ref, da_ref, sums_ref, gb_ref, keep_ref, give_ref,
               middle_s, n2_s, dz_s, acc_s, stage_s, proj_s, sems):
    step = pl.program_id(0)
    last = pl.num_programs(0) - 1
    count, width = x_ref.shape
    core = core_ref[0]
    tile = w1_ref.shape[0]

    @pl.when(step == 0)
    def _():
        middle = x_ref[...].astype(F32) + mm(at_ref[...], wo_ref[...], LAST) + vec_ref[7:8, :]
        middle_s[...] = middle
        unit, _ = norm_parts(middle)
        n2_s[...] = (unit * vec_ref[2:3, :] + vec_ref[3:4, :]).astype(BF16)
        dz_s[...] = jnp.where(live_ref[...] > 0.5, cot_ref[...].astype(F32), 0.0).astype(BF16)
        acc_s[...] = jnp.zeros_like(acc_s)
        dm_ref[...] = jnp.zeros_like(dm_ref)

    slot = lax.rem(step, 2)

    @pl.when(step >= 2)
    def _():
        pltpu.make_async_copy(stage_s.at[slot], stage_s.at[slot], sems.at[slot]).wait()

    n2 = n2_s[...]
    dz = dz_s[...]
    w1 = w1_ref[...]
    w2 = w2_ref[...]
    pre = mm(n2, w1, LAST) + b1_ref[...]
    act, slope = gelu_both(pre)
    hidden = act.astype(BF16)
    acc_s[...] += mm(hidden, w2, PLAIN)
    stage_s[slot, 1] = mm(hidden, dz, FIRST).astype(BF16)
    dpre = (mm(dz, w2, LAST) * slope).astype(BF16)
    gb_ref[...] = jnp.sum(dpre.astype(F32), axis=0, keepdims=True)
    stage_s[slot, 0] = mm(dpre, n2, FIRST).astype(BF16)
    dm_ref[...] += mm(dpre, w1, PLAIN)
    for j in (0, 1):
        send_rows(core, block_rows, stage_s.at[slot, j], (4 + 4 * j) * width + step * tile,
                  base, keep_ref, give_ref, sems.at[slot])

    @pl.when(step == last)
    def _():
        middle = middle_s[...]
        out_ref[...] = (middle + acc_s[...] + vec_ref[12:13, :]).astype(BF16)
        unit, inverse = norm_parts(middle)
        dn = dm_ref[...]
        dy = dz_s[...].astype(F32)
        dm = dy + norm_back(unit, inverse, dn, vec_ref[2:3, :])
        dm_ref[...] = dm
        low = dm.astype(BF16)
        row = lambda a: jnp.sum(a, axis=0, keepdims=True)
        sums_ref[...] = jnp.concatenate(
            [row(dn * unit), row(dn), row(low.astype(F32)), row(dy), jnp.zeros((4, width), F32)], axis=0)
        proj_s[...] = mm(low, at_ref[...], FIRST).astype(BF16)
        send_rows(core, block_rows, proj_s, 3 * width, base, keep_ref, give_ref, sems.at[2])
        da_ref[...] = mm(low, wo_ref[...], PLAIN).astype(BF16)
        pltpu.make_async_copy(stage_s.at[slot], stage_s.at[slot], sems.at[slot]).wait()
        pltpu.make_async_copy(stage_s.at[1 - slot], stage_s.at[1 - slot], sems.at[1 - slot]).wait()
        pltpu.make_async_copy(proj_s, proj_s, sems.at[2]).wait()


def grad_shapes(block_rows, rows, width):
    if block_rows:
        half = jax.ShapeDtypeStruct((rows // block_rows // 2, block_rows, width), BF16)
        return [half, half]
    return [jax.ShapeDtypeStruct((rows, width), BF16), jax.ShapeDtypeStruct((16, width), BF16)]


def mlp(core, x, attn, cot, live, vectors, weights, b1, block_rows, tile=256):
    count, width = x.shape
    units = 4 * width
    stack = weights.shape[0]
    base = 3 * width // block_rows if block_rows else 3 * width
    whole = lambda t: (0, 0)
    big = pl.BlockSpec((count, width), whole)
    hbm = pl.BlockSpec(memory_space=pl.ANY)
    return pl.pallas_call(
        functools.partial(mlp_kernel, block_rows, base),
        grid=(units // tile,),
        in_specs=[pl.BlockSpec(memory_space=pltpu.SMEM), big, big, big, pl.BlockSpec((count, 1), whole),
                  pl.BlockSpec(vectors.shape, whole),
                  pl.BlockSpec((width, width), lambda t: (3, 0)),
                  pl.BlockSpec((tile, width), lambda t: (4 * width // tile + t, 0)),
                  pl.BlockSpec((tile, width), lambda t: (8 * width // tile + t, 0)),
                  pl.BlockSpec((1, tile), lambda t: (0, t))],
        out_specs=[big, big, big, pl.BlockSpec((8, width), whole), pl.BlockSpec((1, tile), lambda t: (0, t)), hbm, hbm],
        out_shape=[
            jax.ShapeDtypeStruct((count, width), BF16),
            jax.ShapeDtypeStruct((count, width), F32),
            jax.ShapeDtypeStruct((count, width), BF16),
            jax.ShapeDtypeStruct((8, width), F32),
            jax.ShapeDtypeStruct((1, units), F32),
        ] + grad_shapes(block_rows, stack - 3 * width, width),
        scratch_shapes=[
            pltpu.VMEM((count, width), F32),
            pltpu.VMEM((count, width), BF16),
            pltpu.VMEM((count, width), BF16),
            pltpu.VMEM((count, width), F32),
            pltpu.VMEM((2, 2, tile, width), BF16),
            pltpu.VMEM((width, width), BF16),
            pltpu.SemaphoreType.DMA((3,)),
        ],
        compiler_params=pltpu.CompilerParams(vmem_limit_bytes=60 * 2**20),
        cost_estimate=pl.CostEstimate(flops=60 * 10**9, bytes_accessed=50 * 10**6, transcendentals=0),
        name="mlp",
    )(core, x, attn, cot, live, vectors, weights, weights, weights, b1)


def back_kernel(block_rows, start, first, final, core_ref, q_ref, k_ref, v_ref, da_ref, at_ref, stat_ref, cos_ref, sin_ref,
                qm_ref, km_ref, pos_ref, n1_ref, wq_ref, wk_ref, wv_ref, *rest):
    if not first:
        before_ref, rest = rest[0], rest[3:]
    if final:
        x_ref, dm_ref, vec_ref = rest[:3]
        rest = rest[3:]
        gb_ref, gf_ref, ig_ref, ln_ref, keep_ref, give_ref, dn_ref, stage_s, sems = rest
    else:
        gb_ref, gf_ref, dn_ref, keep_ref, give_ref, stage_s, sems = rest
    count = q_ref.shape[0]
    width = n1_ref.shape[1]
    step = pl.program_id(0)
    core = core_ref[0]

    @pl.when(step == 0)
    def _():
        dn_ref[...] = jnp.zeros_like(dn_ref) if first else before_ref[...]

    lane = lax.broadcasted_iota(jnp.int32, (1, 128), 1)
    zero = jnp.zeros((), BF16)
    q = q_ref[...]
    k = k_ref[...]
    v = v_ref[...]
    da = da_ref[...]
    prod = da.astype(F32) * at_ref[...].astype(F32)
    qm = qm_ref[...].astype(F32)
    k_aug = jnp.concatenate([k, km_ref[...]], axis=1)
    v_aug = jnp.concatenate([v, jnp.broadcast_to((lane < 2).astype(BF16), (count, 128))], axis=1)
    tile = 256
    dq = dk = dv = None
    for h in (0, 1):
        mine = (lane // 64) == h
        qh = jnp.where(mine, q, zero)
        kh = jnp.where(mine, k, zero)
        dah = jnp.where(mine, da, zero)
        delta = jnp.sum(jnp.where(mine, prod, 0.0), axis=-1, keepdims=True)
        d1, d2, _ = split3(delta)
        l1, l2, l3 = split3(stat_ref[:, 64 * h:64 * h + 1])
        extra = jnp.where(lane == 8, -l1, jnp.where(lane == 9, -l2, jnp.where(lane == 10, -l3, qm)))
        q_aug = jnp.concatenate([qh, extra.astype(BF16)], axis=1)
        da_aug = jnp.concatenate(
            [dah, jnp.where(lane == 0, -d1, jnp.where(lane == 1, -d2, 0.0)).astype(BF16)], axis=1)
        dks, dvs, dqh = [], [], None
        for i in range(count // tile):
            sl = slice(i * tile, (i + 1) * tile)
            p = jnp.exp(mm(k_aug[sl], q_aug, LAST))
            dp = mm(v_aug[sl], da_aug, LAST)
            ds = (p * dp).astype(BF16)
            dvs.append(mm(p.astype(BF16), dah, PLAIN))
            dks.append(mm(ds, qh, PLAIN))
            part = mm(ds, kh[sl], FIRST)
            dqh = part if dqh is None else dqh + part
        dkh = jnp.concatenate(dks, axis=0)
        dvh = jnp.concatenate(dvs, axis=0)
        dq = dqh if dq is None else dq + dqh
        dk = dkh if dk is None else dk + dkh
        dv = dvh if dv is None else dv + dvh
    dq = dq * 0.125
    c = cos_ref[...]
    s = sin_ref[...]
    turned = dq * swap_halves(q.astype(F32) * 8.0) + dk * swap_halves(k.astype(F32))
    turned = jnp.where(lane % 64 < 32, -turned, turned)
    row = lambda a: jnp.sum(a, axis=0, keepdims=True)
    gf_ref[...] = jnp.concatenate(
        [row(turned * pos_ref[:, 0:1]), row(turned * pos_ref[:, 1:2]), jnp.zeros((6, 128), F32)], axis=0)
    dqp = (dq * c - swap_halves(dq) * s).astype(BF16)
    dkp = (dk * c - swap_halves(dk) * s).astype(BF16)
    dvp = dv.astype(BF16)
    gb_ref[...] = jnp.concatenate(
        [row(dqp.astype(F32)), row(dkp.astype(F32)), row(dvp.astype(F32)), jnp.zeros((5, 128), F32)], axis=0)
    d = jnp.concatenate([dqp, dkp, dvp], axis=1)
    w = jnp.concatenate([wq_ref[...], wk_ref[...], wv_ref[...]], axis=0)
    dn_ref[...] += mm(d, w, PLAIN)
    slot = lax.rem(step, 2)

    @pl.when(step >= 2)
    def _():
        pltpu.make_async_copy(stage_s.at[slot], stage_s.at[slot], sems.at[slot]).wait()

    stage_s[slot] = mm(d, n1_ref[...], FIRST).astype(BF16)
    for j in range(3):
        send_rows(core, block_rows, stage_s.at[slot, pl.ds(128 * j, 128)], j * width + (start + step) * 128,
                  0, keep_ref, give_ref, sems.at[slot])

    @pl.when(step == pl.num_programs(0) - 1)
    def _():
        pltpu.make_async_copy(stage_s.at[slot], stage_s.at[slot], sems.at[slot]).wait()
        pltpu.make_async_copy(stage_s.at[1 - slot], stage_s.at[1 - slot], sems.at[1 - slot]).wait()
        if final:
            unit, inverse = norm_parts(x_ref[...].astype(F32))
            dn = dn_ref[...]
            ig_ref[...] = dm_ref[...] + norm_back(unit, inverse, dn, vec_ref[0:1, :])
            ln_ref[...] = jnp.concatenate([row(dn * unit), row(dn), jnp.zeros((6, width), F32)], axis=0)


def attend_back(core, start, stop, before, final, q, k, v, da, attn, stat, cos, sin, qm, km, pos, n1, weights, block_rows):
    count, width = q.shape
    pairs = width // 128
    whole = lambda p: (0, 0)
    col = lambda p: (0, p + start)
    big = pl.BlockSpec((count, width), whole)
    tall = pl.BlockSpec((count, 128), col)
    fixed = pl.BlockSpec((count, 128), whole)
    hbm = pl.BlockSpec(memory_space=pl.ANY)
    w = [pl.BlockSpec((128, width), lambda p, j=j: (p + start + j * pairs, 0)) for j in range(3)]
    small = pl.BlockSpec((8, 128), lambda p: (0, p))
    in_specs = ([pl.BlockSpec(memory_space=pltpu.SMEM)] + [tall] * 8 + [fixed] * 2
                + [pl.BlockSpec((count, 2), whole), big] + w)
    operands = [core, q, k, v, da, attn, stat, cos, sin, qm, km, pos, n1, weights, weights, weights]
    out_specs = [small] * 2
    out_shape = [jax.ShapeDtypeStruct((8, 128 * (stop - start)), F32)] * 2
    dn_shape = jax.ShapeDtypeStruct((count, width), F32)
    scratch = [pltpu.VMEM((2, 384, width), BF16), pltpu.SemaphoreType.DMA((2,))]
    aliases = {}
    if before is not None:
        aliases = {len(operands) + 1: 4 if final else 3, len(operands) + 2: 5 if final else 4}
        in_specs += [big, hbm, hbm]
        operands += list(before)
    if final is not None:
        in_specs += [big, big, pl.BlockSpec(final[2].shape, whole)]
        operands += list(final)
        out_specs += [big, pl.BlockSpec((8, width), whole), hbm, hbm]
        out_shape += [dn_shape, jax.ShapeDtypeStruct((8, width), F32)] + grad_shapes(block_rows, 3 * width, width)
        scratch = [pltpu.VMEM((count, width), F32)] + scratch
    else:
        out_specs += [big, hbm, hbm]
        out_shape += [dn_shape] + grad_shapes(block_rows, 3 * width, width)
    return pl.pallas_call(
        functools.partial(back_kernel, block_rows, start, before is None, final is not None),
        grid=(stop - start,),
        in_specs=in_specs,
        out_specs=out_specs,
        out_shape=out_shape,
        scratch_shapes=scratch,
        input_output_aliases=aliases,
        compiler_params=pltpu.CompilerParams(vmem_limit_bytes=60 * 2**20),
        cost_estimate=pl.CostEstimate(flops=10 * 10**9 * (stop - start), bytes_accessed=30 * 10**6, transcendentals=0),
        name="attend_back",
    )(*operands)


def fold_kernel(pos_ref, *refs):
    keep, got, send_ref, hold_ref = refs[:4], refs[4:8], refs[8], refs[9]
    for k in range(4):
        out = (send_ref, hold_ref)[k // 2]
        out[k % 2, 0] = (keep[k][0].astype(F32) + got[k][0].astype(F32)).astype(BF16)


def fold(pos, keep, got):
    count, rows, width = keep.shape
    quarter = [pl.BlockSpec((1, rows // 2, width // 2), lambda i, pos, k=k: (i, pos[k, 0], pos[k, 1])) for k in range(4)]
    out = pl.BlockSpec((2, 1, rows // 2, width // 2), lambda i, pos: (0, i, 0, 0))
    shape = jax.ShapeDtypeStruct((2, count, rows // 2, width // 2), BF16)
    return pl.pallas_call(
        fold_kernel,
        grid_spec=pltpu.PrefetchScalarGridSpec(
            num_scalar_prefetch=1, grid=(count,), in_specs=quarter * 2, out_specs=[out, out]),
        out_shape=[shape, shape],
        name="fold",
    )(pos, *([keep] * 4), *([got] * 4))


def adam_kernel(scal_ref, a_ref, b_ref, w_ref, m_ref, v_ref, g_out, v_out, w_out):
    clip = scal_ref[0]
    own = scal_ref[1] > 0.5
    grad = jnp.where(own, a_ref[:, 0, 0].astype(F32), b_ref[:, 0, 0].astype(F32))
    grad = grad[:, :w_ref.shape[0] // grad.shape[0]].reshape(w_ref.shape) * clip
    second, weight = adam(w_ref[...], m_ref[...], v_ref[...], grad, 0.02, 0.05)
    g_out[...] = grad
    v_out[...] = second
    w_out[...] = weight


def adam_rows(scal, mine, other, weight, first, second):
    rows, width = weight.shape
    deep, tall, wide, piece, cols = mine.shape
    part = pl.BlockSpec((deep, 1, 1, piece, cols), lambda y, x: (0, y, x, 0, 0))
    flat = pl.BlockSpec((rows // tall, width // wide), lambda y, x: (y, x))
    shape = jax.ShapeDtypeStruct((rows, width), F32)
    return pl.pallas_call(
        adam_kernel,
        grid=(tall, wide),
        in_specs=[pl.BlockSpec(memory_space=pltpu.SMEM), part, part, flat, flat, flat],
        out_specs=[flat] * 3,
        out_shape=[shape] * 3,
        name="adam",
    )(scal, mine, other, weight, first, second)


from jax.sharding import PartitionSpec as P

HEADS = 12
STEP = 7


def place_tokens(heights, widths, count):
    sizes = heights * widths
    ends = jnp.cumsum(sizes)
    starts = ends - sizes
    places = jnp.arange(count, dtype=jnp.int32)
    segment = jnp.sum((places[:, None] >= ends[None, :]).astype(jnp.int32), axis=1)
    slots = jnp.arange(heights.shape[0], dtype=jnp.int32)
    picks = (segment[:, None] == slots[None, :]).astype(jnp.int32)
    begin = jnp.sum(picks * starts[None, :], axis=1)
    across = jnp.maximum(jnp.sum(picks * widths[None, :], axis=1), 1)
    offset = places - begin
    live = places < ends[-1]
    return (segment, offset // across, offset % across, live)


def adam(weight, first, second, grad, rate, decay):
    first_new = 0.5 * first + 0.5 * grad
    second_new = 0.5 * second + 0.5 * grad * grad
    correct = 1.0 - 0.5**STEP
    direction = first_new / correct / (jnp.sqrt(second_new / correct) + 1e-08)
    return (second_new, weight - rate * (direction + decay * weight))


def pairwise(bits, total):
    return [(i, i ^ bits) for i in range(total)]


def sum_everywhere(value, devices):
    if devices & (devices - 1):
        return lax.psum(value, "dp")
    step = 1
    while step < devices:
        value = value + lax.ppermute(value, "dp", pairwise(step, devices))
        step *= 2
    return value


CORES = ("group", "dp")
SWAP = [(0, 1), (1, 0)]


def cross(value, bit0, bit1, devices):
    perm = [(i, i ^ (bit0 if i < devices else bit1)) for i in range(2 * devices)]
    return lax.ppermute(value, CORES, perm)


def along_z(values, devices):
    return [
        lax.ppermute(v, "dp", [(i, (i + 4 * (s + 1)) % devices) for i in range(devices)])
        for s, v in enumerate(values)
    ]


def gather_pieces(master, inverse, core, me, devices, tables):
    block_rows, width = master.shape
    half = block_rows // 2
    mine = lax.dynamic_slice_in_dim(master, core * half, half, 0).astype(BF16)
    large = mine[:LARGE]
    small = mine[LARGE:]
    up = along_z([large] * 3, devices)
    small = jnp.stack([small, cross(small, 1, 2, devices)])
    small = jnp.concatenate([small, cross(small, 2, 1, devices)])
    large = jnp.stack([large] + up)
    large, small, tables = lax.optimization_barrier((large, small, tables))
    first = jnp.concatenate([large, cross(large, 1, 2, devices)])
    small = jnp.concatenate([small] + along_z([small] * 3, devices))
    second = cross(first, 2, 1, devices)
    other = [lax.ppermute(a, "group", SWAP) for a in (first, second, small)]
    deep = lax.rem(me // 4 - inverse // 4 + 4, 4)
    apart = me ^ inverse
    one = jnp.where(core == 0, apart & 1, (apart >> 1) & 1)
    two = jnp.where(core == 0, (apart >> 1) & 1, apart & 1)
    slots = jnp.stack([
        8 * two + 4 * one + deep,
        4 * deep + 2 * two + one,
        8 * one + 4 * two + deep,
        4 * deep + 2 * one + two,
    ]).astype(jnp.int32)
    return (first, second, small, *other), slots, tables


def reduce_blocks(keep, give, core, me, devices):
    count, rows, width = keep.shape
    x, y, z = me & 1, (me >> 1) & 1, me // 4
    one = jnp.where(core == 0, x, y)
    two = jnp.where(core == 0, y, x)
    pairs = [(1 - one, 1 - two), (1 - one, two), (one, 1 - two), (one, two)]
    pos = jnp.stack([
        jnp.stack([jnp.where(core == 0, b, a), jnp.where(core == 0, a, b)]) for a, b in pairs
    ]).astype(jnp.int32)
    got = lax.ppermute(give, "group", SWAP)
    send, hold = fold(pos, keep, got)
    came = cross(send, 1, 2, devices)

    def add(a, b):
        return a.astype(F32) + b.astype(F32)

    again = cross(add(hold[0], came[0]).astype(BF16), 2, 1, devices)
    total = add(add(hold[1], came[1]), again).reshape(count, 4, rows // 8, width // 2)
    low = total.astype(BF16)
    pick = lambda a, at: lax.dynamic_index_in_dim(a, at, 1, keepdims=False)
    parts = along_z([pick(low, lax.rem(z + s, 4)) for s in (1, 2, 3)], devices)
    total = pick(total, z)
    for part in parts:
        total = add(total, part)
    return total


def share_blocks(total, owner_block, core, devices):
    blocks, rows, cols = total.shape
    square = jnp.sum(total * total)
    lane = jnp.arange(cols)
    one, two, three = split3(square)
    extra = jnp.where(lane == 0, one, jnp.where(lane == 1, two, jnp.where(lane == 2, three, 0.0)))
    extra = jnp.broadcast_to(extra.astype(BF16), (devices, 8, cols))
    load = jnp.concatenate([total.astype(BF16)[owner_block // 2], extra], axis=1)
    mine = lax.all_to_all(load, "dp", 0, 0, tiled=True)
    other = lax.ppermute(mine, "group", SWAP)

    def squares(a):
        return jnp.sum(a[:, rows, :3].astype(F32))

    shape = (4, 2, 2, rows + 8, cols)
    return mine.reshape(shape), other.reshape(shape), squares(mine) + squares(other)


def reduce_plain(local_mat, owner_block, devices):
    rows, width = local_mat.shape
    block_rows = rows // devices
    term = local_mat.reshape(devices, block_rows, width)[owner_block].reshape(rows, width)
    share = lax.psum_scatter(term.astype(F32), "dp", scatter_dimension=0, tiled=True)
    return lax.psum(share.astype(BF16), "group").astype(F32)


def local(
    tokens,
    cotangent,
    grid_h,
    grid_w,
    owner_block,
    master,
    first_mom,
    second_mom,
    vectors,
    vec_first,
    vec_second,
):
    devices = lax.axis_size("dp")
    core = lax.axis_index("group")
    me = lax.axis_index("dp")
    count = tokens.shape[1]
    width = tokens.shape[2]
    heads = HEADS
    head_dim = width // heads
    half = head_dim // 2
    block_rows = master.shape[0]
    stack = devices * block_rows
    quick = devices == 16 and block_rows == 2 * (LARGE + SMALL) and width % 256 == 0
    inverse = jnp.argsort(owner_block)
    segment, rows_pos, cols_pos, live = place_tokens(grid_h[0], grid_w[0], count)
    freqs = vectors[13]

    def spread(part):
        return jnp.broadcast_to(part.reshape(heads, 1, half), (heads, 2, half)).reshape(1, width)

    angle = rows_pos.astype(F32)[:, None] * spread(freqs[: width // 2]) + cols_pos.astype(F32)[
        :, None
    ] * spread(freqs[width // 2 :])
    lower = (jnp.arange(width) % head_dim < half)[None]
    cosine = jnp.cos(angle)
    sine = jnp.sin(angle)
    sine = jnp.where(lower, -sine, sine)
    ids = jnp.arange(128)[None]
    match = segment[:, None] == ids
    key_mask = jnp.where(match | ((ids >= 8) & (ids < 11)), 1.0, 0.0).astype(BF16)
    query_mask = jnp.where((ids < 8) & ~match, MASKED, 0.0).astype(BF16)
    places = jnp.stack([rows_pos, cols_pos], axis=1).astype(F32)
    alive = live[:, None].astype(F32)
    tables = (cosine, sine, key_mask, query_mask, places, alive)
    if quick:
        weights, slots, tables = gather_pieces(master, inverse, core, me, devices, tables)
    else:
        low = lax.all_gather(master.astype(BF16), "dp", axis=0, tiled=True)
        weights = low.reshape(devices, block_rows, width)[inverse].reshape(stack, width)
        slots = jnp.zeros((4, devices), jnp.int32)
    cosine, sine, key_mask, query_mask, places, alive = tables
    here = core.reshape(1).astype(jnp.int32)
    x = tokens[0]
    first_in, query, key, value, attn, stat, *placed = attend(
        here, slots, x, vectors[0:1], vectors[1:2], vectors[4:7].reshape(1, 3 * width),
        cosine, sine, query_mask, key_mask, weights, stack,
    )
    if quick:
        weights = placed[0]
    whole_rows = block_rows if quick else 0
    block_out, grad_middle, grad_attn, sums, bias_up, keep_mlp, give_mlp = mlp(
        here, x, attn, cotangent[0], alive, vectors, weights, vectors[8:12].reshape(1, 4 * width), whole_rows
    )
    if quick:
        late = reduce_blocks(keep_mlp, give_mlp, core, me, devices)
    pairs = width // 128
    fixed = (query, key, value, grad_attn, attn, stat, cosine, sine, query_mask, key_mask, places, first_in, weights)
    cut = pairs // 2
    gb1, gf1, *before = attend_back(here, 0, cut, None, None, *fixed, whole_rows)
    gb2, gf2, input_grad, norm_sums, keep_qkv, give_qkv = attend_back(
        here, cut, pairs, before, (x, grad_middle, vectors), *fixed, whole_rows
    )
    grad_bias = jnp.concatenate([gb1, gb2], axis=1)
    grad_freq = jnp.concatenate([gf1, gf2], axis=1)
    grad_freqs = grad_freq[:2].reshape(2, heads, 2, half).sum(2).reshape(1, width)
    local_vec = jnp.concatenate(
        [norm_sums[:2], sums[:2], grad_bias[:3], sums[2:3], bias_up.reshape(4, width), sums[3:4], grad_freqs],
        axis=0,
    )
    if quick:
        early = reduce_blocks(keep_qkv, give_qkv, core, me, devices)
        vec_total = sum_everywhere(local_vec + lax.ppermute(local_vec, "group", SWAP), devices)
        total = jnp.concatenate([early, late])
        mine, other, square = share_blocks(total, owner_block, core, devices)
    else:
        vec_total = lax.psum(local_vec, CORES)
        share = reduce_plain(jnp.concatenate([keep_qkv, keep_mlp]), owner_block, devices)
        square = lax.psum(jnp.sum(share * share), "dp")
    grad_norm = jnp.sqrt(square + jnp.sum(vec_total * vec_total))
    clip = jnp.minimum(1.0, 1.0 / (grad_norm + 1e-06))
    vec_grad = vec_total * clip
    vec_second_new, vec_weight = adam(vectors, vec_first, vec_second, vec_grad, 0.2, 0.0)
    if quick:
        own = (owner_block[me] % 2 == core).astype(F32)
        mat_grad, mat_second, mat_weight = adam_rows(
            jnp.stack([clip, own]), mine, other, master, first_mom, second_mom
        )
    else:
        mat_grad = share * clip
        mat_second, mat_weight = adam(master, first_mom, second_mom, mat_grad, 0.02, 0.05)
    return (
        block_out[None],
        input_grad[None],
        mat_grad,
        mat_second,
        mat_weight,
        vec_grad,
        vec_second_new,
        vec_weight,
        grad_norm,
    )


def solution(mesh):
    return jax.shard_map(
        local,
        mesh=mesh,
        in_specs=(
            P("group", "dp", None),
            P("group", "dp", None),
            P("group", "dp"),
            P("group", "dp"),
            P(),
            P("dp", None),
            P("dp", None),
            P("dp", None),
            P(),
            P(),
            P(),
        ),
        out_specs=(
            P("group", "dp", None),
            P("group", "dp", None),
            P("dp", None),
            P("dp", None),
            P("dp", None),
            P(),
            P(),
            P(),
            P(),
        ),
        check_vma=False,
    )
```

time: 536 us -> 845 us (1.58)
  Pallas kernels: 139 us -> 591 us
  local copies, waits for them, and re-layouts: 69.9 us -> 13 us
  waiting for transfers between devices: 194 us -> 138 us
  other arithmetic: 73.2 us -> 32.8 us
  starting transfers between devices: 27.4 us -> 54.2 us
  between operations: 20.1 us -> 8 us
  matrix products: 8.55 us -> 0 us
    pallas_call x3 -> x7, Pallas kernels: 139 us -> 591 us  [the longest x1 434 us: attend(): pl.pallas_call(functools.partial(attend_kernel, blocks), grid=(pairs,), i...]
    all_gather x1 -> x0, waiting for transfers between devices: 106 us -> none  [gather_weights(): lax.all_gather(lax.dynamic_slice_in_dim(low, core * half, half, 0), 'dp',...]
    ppermute x9 -> x27, waiting for transfers between devices: 60.8 us -> 108 us  [the longest x8 69.8 us: cross(): return lax.ppermute(value, CORES, perm)]
    ppermute x9 -> x27, starting transfers between devices: 8.02 us -> 43 us  [the longest x12 29.9 us: along_z(): lax.ppermute(v, 'dp', [(i, (i + 4 * (s + 1)) % devices) for i in range(de...]
    gather x5 -> x1, local copies, waits for them, and re-layouts: 32.1 us -> 0.75 us  [share_blocks(): total.astype(BF16)[owner_block // 2]]
    all_to_all x0 -> x1, waiting for transfers between devices: none -> 21.4 us  [share_blocks(): mine = lax.all_to_all(load, 'dp', 0, 0, tiled=True)]
    ppermute x8 -> x4, waiting for transfers between devices: 26.9 us -> 8.54 us  [sum_everywhere(): value = value + lax.ppermute(value, 'dp', pairwise(step, devices))]
    slice x5 -> x4, local copies, waits for them, and re-layouts: 14.2 us -> 1.34 us  [the longest x1 0.74 us: local(): norm_sums[:2]]
  transfers between devices with their start and end apart: 18 -> 32, of which waited for: 13 -> 17; matrix products, arithmetic and copies ran while one was open for 10% -> 4% of each run, Pallas kernels for 0% -> 9%
where the time goes in v2:
time: 845 us; the launch traced here: 836 us
  Pallas kernels  591 us (70%)
  waiting for transfers between devices  138 us (16%)
  starting transfers between devices  54.2 us (6%)
  other arithmetic  32.8 us (4%)
  local copies, waits for them, and re-layouts  13 us (2%)
    pallas_call x1, Pallas kernels, attend(): pl.pallas_call(functools.partial(attend_kernel, blocks), grid=(pairs,), i...  434 us
    ppermute x8, waiting for transfers between devices, cross(): return lax.ppermute(value, CORES, perm)  69.8 us
    pallas_call x2, Pallas kernels, attend_back(): pl.pallas_call(functools.partial(back_kernel, block_rows, start, before i...  68.8 us
    pallas_call x1, Pallas kernels, mlp(): pl.pallas_call(functools.partial(mlp_kernel, block_rows, base), grid=(uni...  68.6 us
    ppermute x12, waiting for transfers between devices, along_z(): lax.ppermute(v, 'dp', [(i, (i + 4 * (s + 1)) % devices) for i in range(de...  32.4 us
    ppermute x12, starting transfers between devices, along_z(): lax.ppermute(v, 'dp', [(i, (i + 4 * (s + 1)) % devices) for i in range(de...  29.9 us
    all_to_all x1, waiting for transfers between devices, share_blocks(): mine = lax.all_to_all(load, 'dp', 0, 0, tiled=True)  21.4 us
  transfers between devices with their start and end apart: 32, of which 17 were waited for; matrix products, arithmetic and copies ran while one was open for 4% of the time, Pallas kernels for 9%

profile of v2, /device:TPU:0, one launch (start us, length us, event | category | flops | bytes accessed | tf_op | source)
XLA Modules:
  0.0 836.4 jit_solution(16480030830675968187)
XLA Ops:
  2.0 4.1 collective-permute-start.1
  13.5 13.0 %negate_select_fusion = (f32[1024,768]{1,0:T(8,128)}, f32[1024,768]{1,0:T(8,128)}) fusion(f32[768]{0:T(1024)S(1)} %mul.147, f32[1024]{0:T(1024)S(1)} %get-tuple-element.123, f32[768]{0:T(1024)S(1)} %mul.143, f32[1024]{0:T(1024)S(1)} %get-tuple-element.122, pred[768]{0:T(1024)(128)(4,1)S(1)} %fusion.22), kind=kLoop, calls=%fused_computation.1 | loop fusion | flops 3932160 | bytes 6306560 | tf_op jit(solution)/shard_map/jit(_where)/select_n | solution.py:724
  32.1 3.0 collective-permute-done.4
  35.8 16.8 %collective-permute-done.5 = bf16[4,208,768]{2,1,0:T(8,128)(2,1)S(1)} collective-permute-done((bf16[4,208,768]{2,1,0:T(8,128)(2,1)S(1)}, bf16[4,208,768]{2,1,0:T(8,128)(2,1)S(1)}, u32[]{:S(2)}, u32[]{:S(2)}) %collective-permute-start.5) | collective-permute-done | bytes 1277984 | tf_op jit(solution)/shard_map/ppermute | solution.py:596
  52.7 3.3 collective-permute-start.6
  56.0 3.8 collective-permute-start.9
  59.9 25.2 %collective-permute-done.6.rest_1_ = bf16[8,208,768]{2,1,0:T(8,128)(2,1)} collective-permute-done((bf16[8,208,768]{2,1,0:T(8,128)(2,1)S(1)}, bf16[8,208,768]{2,1,0:T(8,128)(2,1)}, u32[]{:S(2)}, u32[]{:S(2)}) %collective-permute-start.6) | collective-permute-done | bytes 2555936 | tf_op jit(solution)/shard_map/ppermute | solution.py:596
  93.1 434.1 %attend.1 = (bf16[1024,768]{1,0:T(8,128)(2,1)}, bf16[1024,768]{1,0:T(8,128)(2,1)}, bf16[1024,768]{1,0:T(8,128)(2,1)}, bf16[1024,768]{1,0:T(8,128)(2,1)}, bf16[10...) custom-call(s32[1]{0:T(128)} %bitcast.core_ref, s32[4,16]{1,0:T(4,128)} %pad_add_fusion.1.slot_ref, ...), custom_call_target="tpu_custom_call" | custom-call | flops 30000001024 | bytes 40000000 | tf_op jit(solution)/shard_map/attend/pallas_call | solution.py:186
  527.2 68.6 %mlp.1 = (bf16[1024,768]{1,0:T(8,128)(2,1)}, f32[1024,768]{1,0:T(8,128)}, bf16[1024,768]{1,0:T(8,128)(2,1)}, f32[8,768]{1,0:T(8,128)}, f32[1,3072]{1,0:T(1,128)}...) custom-call(s32[1]{0:T(128)} %bitcast.core_ref, bf16[1024,768]{1,0:T(8,128)(2,1)} %bitcast.117, ...), custom_call_target="tpu_custom_call" | custom-call | flops 60000002048 | bytes 50000000 | tf_op jit(solution)/shard_map/mlp/pallas_call | solution.py:325
  596.7 32.1 %attend_back.2 = (f32[8,384]{1,0:T(8,128)}, f32[8,384]{1,0:T(8,128)}, f32[1024,768]{1,0:T(8,128)}, bf16[2,576,768]{2,1,0:T(8,128)(2,1)}, bf16[2,576,768]{2,1,0:T(8,128)(2,1)}) custom-call(s32[1]{0:T(128)} %bitcast.core_ref, bf16[1024,768]{1,0:T(8,128)(2,1)} %get-tuple-element.61.q_ref, bf16[1024,768]{1,0:T(8,128)(2,1)} %get-tuple-element.62.k_ref, ...), custom_call_target="tpu_custom_call" | custom-call | flops 30000001024 | bytes 30000000 | tf_op jit(solution)/shard_map/attend_back/pallas_call | solution.py:485
  628.8 8.6 %fold.3 = (bf16[2,6,288,384]{3,2,1,0:T(8,128)(2,1)}, bf16[2,6,288,384]{3,2,1,0:T(8,128)(2,1)}) custom-call(s32[4,2]{1,0:T(4,128)} %pad_add_fusion.2.pos_ref, bf16[6,576,768]{2,1,0:T(8,128)(2,1)} %get-tuple-element.77.refs_0_.refs_1_.refs_2_.refs_3_, bf16[6,576,768]{2,1,0:T(8,128)(2,1)} %get-tuple-element.77.refs_0_.refs_1_.refs_2_.refs_3_, ...), custom_call_target="tpu_custom_call" | custom-call | tf_op jit(solution)/shard_map/fold/pallas_call | solution.py:511
  637.9 36.8 %attend_back.3 = (f32[8,384]{1,0:T(8,128)}, f32[8,384]{1,0:T(8,128)}, f32[1024,768]{1,0:T(8,128)}, f32[8,768]{1,0:T(8,128)}, bf16[2,576,768]{2,1,0:T(8,128)(2,1)}, /*index=5*/bf16[2,576,768]{2,1,0:T(8,128)(2,1)}) custom-call(s32[1]{0:T(128)} %bitcast.core_ref, ...), custom_call_target="tpu_custom_call", output_to_operand_aliasing={{4}: (17, {}), {5}: (18, {})} | custom-call | flops 30000001024 | bytes 30000000 | tf_op jit(solution)/shard_map/attend_back/pallas_call | solution.py:485
  676.3 3.5 collective-permute-done.13.refs_4_.refs_5_.refs_6_.refs_7_
  681.0 4.2 fold.2
  689.9 16.5 %collective-permute-done.14 = bf16[2,2,288,384]{3,2,1,0:T(8,128)(2,1)S(1)} collective-permute-done((bf16[2,2,288,384]{3,2,1,0:T(8,128)(2,1)}, bf16[2,2,288,384]{3,2,1,0:T(8,128)(2,1)S(1)}, u32[]{:S(2)}, u32[]{:S(2)}) %collective-permute-start.14) | collective-permute-done | bytes 884768 | tf_op jit(solution)/shard_map/ppermute | solution.py:596
  708.6 8.4 %collective-permute-done.15 = bf16[2,288,384]{2,1,0:T(8,128)(2,1)} collective-permute-done((bf16[2,288,384]{2,1,0:T(8,128)(2,1)}, bf16[2,288,384]{2,1,0:T(8,128)(2,1)}, u32[]{:S(2)}, u32[]{:S(2)}) %collective-permute-start.15) | collective-permute-done | bytes 442400 | tf_op jit(solution)/shard_map/ppermute | solution.py:596
  718.4 10.2 %collective-permute-start.16 = (bf16[2,72,384]{2,1,0:T(8,128)(2,1)S(1)}, bf16[2,72,384]{2,1,0:T(8,128)(2,1)S(1)}, u32[]{:S(2)}, u32[]{:S(2)}) collective-permute-start(bf16[2,72,384]{2,1,0:T(8,128)(2,1)S(1)} %get-tuple-element.107), channel_id=1, source_target_pairs={{0,4},{1,5},{2,6},{3,7},{4,8},{5,9},{6,10},{7,11},{8,12},{9,13},{1... | collective-permute-start | bytes 331784 | tf_op jit(solution)/shard_map/ppermute | solution.py:601
  738.6 10.8 %collective-permute-done.17 = bf16[2,72,384]{2,1,0:T(8,128)(2,1)S(1)} collective-permute-done((bf16[2,72,384]{2,1,0:T(8,128)(2,1)S(1)}, bf16[2,72,384]{2,1,0:T(8,128)(2,1)S(1)}, u32[]{:S(2)}, u32[]{:S(2)}) %collective-permute-start.17) | collective-permute-done | bytes 110624 | tf_op jit(solution)/shard_map/ppermute | solution.py:601
  749.5 5.0 collective-permute-done.24
  754.5 16.2 %collective-permute-done.23 = bf16[6,72,384]{2,1,0:T(8,128)(2,1)S(1)} collective-permute-done((bf16[6,72,384]{2,1,0:T(8,128)(2,1)S(1)}, bf16[6,72,384]{2,1,0:T(8,128)(2,1)S(1)}, u32[]{:S(2)}, u32[]{:S(2)}) %collective-permute-start.23) | collective-permute-done | bytes 331808 | tf_op jit(solution)/shard_map/ppermute | solution.py:601
  775.0 4.0 all-to-all-start
  781.0 21.4 %all-to-all-done = bf16[16,80,384]{2,1,0:T(8,128)(2,1)S(1)} async-done(((bf16[16,80,384]{2,1,0:T(8,128)(2,1)}), bf16[16,80,384]{2,1,0:T(8,128)(2,1)S(1)}, u32[]{:S(2)}, u32[]{:S(2)}) %all-to-all-start) | async-done | bytes 983072 | tf_op jit(solution)/shard_map/all_to_all | solution.py:669
  805.7 3.5 collective-permute-done.27
  828.6 6.2 adam.1
  (177 shorter events, 69.1 us)
Async XLA Ops:
  2.0 29.9 %collective-permute-start.1 = (bf16[208,768]{1,0:T(8,128)(2,1)S(1)}, bf16[208,768]{1,0:T(8,128)(2,1)S(1)}, u32[]{:S(2)}, u32[]{:S(2)}) collective-permute-start(bf16[208,768]{1,0:T(8,128)(2,1)S(1)} %get-tuple-element.113), channel_id=1, source_target_pairs={{0,8},{1,9},{2,10},{3,11},{4,12},{5,13},{6,14},{7,15},{8,0},{9,1},... | collective-permute-start | bytes 958472 | tf_op jit(solution)/shard_map/ppermute | solution.py:601
  6.1 25.8 %collective-permute-start = (bf16[208,768]{1,0:T(8,128)(2,1)S(1)}, bf16[208,768]{1,0:T(8,128)(2,1)S(1)}, u32[]{:S(2)}, u32[]{:S(2)}) collective-permute-start(bf16[208,768]{1,0:T(8,128)(2,1)S(1)} %get-tuple-element.113), channel_id=1, source_target_pairs={{0,4},{1,5},{2,6},{3,7},{4,8},{5,9},{6,10},{7,11},{8,12},{9,13},{1... | collective-permute-start | bytes 958472 | tf_op jit(solution)/shard_map/ppermute | solution.py:601
  7.6 24.3 %collective-permute-start.2 = (bf16[208,768]{1,0:T(8,128)(2,1)S(1)}, bf16[208,768]{1,0:T(8,128)(2,1)S(1)}, u32[]{:S(2)}, u32[]{:S(2)}) collective-permute-start(bf16[208,768]{1,0:T(8,128)(2,1)S(1)} %get-tuple-element.113), channel_id=1, source_target_pairs={{0,12},{1,13},{2,14},{3,15},{4,0},{5,1},{6,2},{7,3},{8,4},{9,5},{1... | collective-permute-start | bytes 958472 | tf_op jit(solution)/shard_map/ppermute | solution.py:601
  9.9 18.9 %collective-permute-start.3 = (bf16[80,768]{1,0:T(8,128)(2,1)S(1)}, bf16[80,768]{1,0:T(8,128)(2,1)S(1)}, u32[]{:S(2)}, u32[]{:S(2)}) collective-permute-start(bf16[80,768]{1,0:T(8,128)(2,1)S(1)} %get-tuple-element.111), channel_id=1, source_target_pairs={{0,1},{1,0},{2,3},{3,2},{4,5},{5,4},{6,7},{7,6},{8,9},{9,8},{10,11... | collective-permute-start | bytes 368648 | tf_op jit(solution)/shard_map/ppermute | solution.py:596
  35.1 17.4 %collective-permute-start.5 = (bf16[4,208,768]{2,1,0:T(8,128)(2,1)S(1)}, bf16[4,208,768]{2,1,0:T(8,128)(2,1)S(1)}, u32[]{:S(2)}, u32[]{:S(2)}) collective-permute-start(bf16[4,208,768]{2,1,0:T(8,128)(2,1)S(1)} %pad_maximum_fusion), channel_id=1, source_target_pairs={{0,1},{1,0},{2,3},{3,2},{4,5},{5,4},{6,7},{7,6},{8,9},{9,8},{10,11... | collective-permute-start | bytes 3833864 | tf_op jit(solution)/shard_map/ppermute | solution.py:596
  52.7 32.4 %collective-permute-start.6 = (bf16[8,208,768]{2,1,0:T(8,128)(2,1)S(1)}, bf16[8,208,768]{2,1,0:T(8,128)(2,1)}, u32[]{:S(2)}, u32[]{:S(2)}) collective-permute-start(bf16[8,208,768]{2,1,0:T(8,128)(2,1)S(1)} %constant_dynamic-update-slice_fusion.rest_0_), channel_id=1, source_target_pairs={{0,2},{1,3},{2,0},{3,1},{4,6},{5,7},{6,4},{7,5},{8,10},{9,11},{10,... | collective-permute-start | bytes 7667720 | tf_op jit(solution)/shard_map/ppermute | solution.py:596
  56.0 29.9 %collective-permute-start.7 = (bf16[4,80,768]{2,1,0:T(8,128)(2,1)S(1)}, bf16[4,80,768]{2,1,0:T(8,128)(2,1)S(1)}, u32[]{:S(2)}, u32[]{:S(2)}) collective-permute-start(bf16[4,80,768]{2,1,0:T(8,128)(2,1)S(1)} %pad_maximum_fusion.3), channel_id=1, source_target_pairs={{0,4},{1,5},{2,6},{3,7},{4,8},{5,9},{6,10},{7,11},{8,12},{9,13},{1... | collective-permute-start | bytes 1474568 | tf_op jit(solution)/shard_map/ppermute | solution.py:601
  56.0 31.0 %collective-permute-start.8 = (bf16[4,80,768]{2,1,0:T(8,128)(2,1)S(1)}, bf16[4,80,768]{2,1,0:T(8,128)(2,1)S(1)}, u32[]{:S(2)}, u32[]{:S(2)}) collective-permute-start(bf16[4,80,768]{2,1,0:T(8,128)(2,1)S(1)} %pad_maximum_fusion.3), channel_id=1, source_target_pairs={{0,8},{1,9},{2,10},{3,11},{4,12},{5,13},{6,14},{7,15},{8,0},{9,1},... | collective-permute-start | bytes 1474568 | tf_op jit(solution)/shard_map/ppermute | solution.py:601
  56.0 31.9 %collective-permute-start.9 = (bf16[4,80,768]{2,1,0:T(8,128)(2,1)S(1)}, bf16[4,80,768]{2,1,0:T(8,128)(2,1)S(1)}, u32[]{:S(2)}, u32[]{:S(2)}) collective-permute-start(bf16[4,80,768]{2,1,0:T(8,128)(2,1)S(1)} %pad_maximum_fusion.3), channel_id=1, source_target_pairs={{0,12},{1,13},{2,14},{3,15},{4,0},{5,1},{6,2},{7,3},{8,4},{9,5},{1... | collective-permute-start | bytes 1474568 | tf_op jit(solution)/shard_map/ppermute | solution.py:601
  59.9 33.2 %collective-permute-start.10 = (bf16[8,208,768]{2,1,0:T(8,128)(2,1)S(1)}, bf16[8,208,768]{2,1,0:T(8,128)(2,1)}, u32[]{:S(2)}, u32[]{:S(2)}) collective-permute-start(bf16[8,208,768]{2,1,0:T(8,128)(2,1)S(1)} %constant_dynamic-update-slice_fusion.rest_0_), channel_id=1, source_target_pairs={{0,16},{16,0},{1,17},{17,1},{2,18},{18,2},{3,19},{19,3},{4,20},{20... | collective-permute-start | bytes 7667720 | tf_op jit(solution)/shard_map/ppermute | solution.py:620
  85.1 8.0 collective-permute-start.11
  595.8 33.0 %collective-permute-start.19 = (bf16[6,576,768]{2,1,0:T(8,128)(2,1)}, bf16[6,576,768]{2,1,0:T(8,128)(2,1)}, u32[]{:S(2)}, u32[]{:S(2)}) collective-permute-start(bf16[6,576,768]{2,1,0:T(8,128)(2,1)} %get-tuple-element.78), channel_id=1, source_target_pairs={{0,16},{16,0},{1,17},{17,1},{2,18},{18,2},{3,19},{19,3},{4,20},{20... | collective-permute-start | bytes 15925256 | tf_op jit(solution)/shard_map/ppermute | solution.py:643
  637.4 48.3 %collective-permute-start.20 = (bf16[2,6,288,384]{3,2,1,0:T(8,128)(2,1)}, bf16[2,6,288,384]{3,2,1,0:T(8,128)(2,1)}, u32[]{:S(2)}, u32[]{:S(2)}) collective-permute-start(bf16[2,6,288,384]{3,2,1,0:T(8,128)(2,1)} %get-tuple-element.80), channel_id=1, source_target_pairs={{0,1},{1,0},{2,3},{3,2},{4,5},{5,4},{6,7},{7,6},{8,9},{9,8},{10,11... | collective-permute-start | bytes 7962632 | tf_op jit(solution)/shard_map/ppermute | solution.py:596
  685.2 21.2 %collective-permute-start.14 = (bf16[2,2,288,384]{3,2,1,0:T(8,128)(2,1)}, bf16[2,2,288,384]{3,2,1,0:T(8,128)(2,1)S(1)}, u32[]{:S(2)}, u32[]{:S(2)}) collective-permute-start(bf16[2,2,288,384]{3,2,1,0:T(8,128)(2,1)} %get-tuple-element.76), channel_id=1, source_target_pairs={{0,1},{1,0},{2,3},{3,2},{4,5},{5,4},{6,7},{7,6},{8,9},{9,8},{10,11... | collective-permute-start | bytes 2654216 | tf_op jit(solution)/shard_map/ppermute | solution.py:596
  687.8 44.2 %collective-permute-start.21 = (bf16[6,288,384]{2,1,0:T(8,128)(2,1)S(1)}, bf16[6,288,384]{2,1,0:T(8,128)(2,1)S(1)}, u32[]{:S(2)}, u32[]{:S(2)}) collective-permute-start(bf16[6,288,384]{2,1,0:T(8,128)(2,1)S(1)} %fusion.1), channel_id=1, source_target_pairs={{0,2},{1,3},{2,0},{3,1},{4,6},{5,7},{6,4},{7,5},{8,10},{9,11},{10,... | collective-permute-start | bytes 3981320 | tf_op jit(solution)/shard_map/ppermute | solution.py:596
  708.2 8.8 %collective-permute-start.15 = (bf16[2,288,384]{2,1,0:T(8,128)(2,1)}, bf16[2,288,384]{2,1,0:T(8,128)(2,1)}, u32[]{:S(2)}, u32[]{:S(2)}) collective-permute-start(bf16[2,288,384]{2,1,0:T(8,128)(2,1)} %fusion.9), channel_id=1, source_target_pairs={{0,2},{1,3},{2,0},{3,1},{4,6},{5,7},{6,4},{7,5},{8,10},{9,11},{10,... | collective-permute-start | bytes 1327112 | tf_op jit(solution)/shard_map/ppermute | solution.py:596
  718.4 19.6 %collective-permute-start.16 = (bf16[2,72,384]{2,1,0:T(8,128)(2,1)S(1)}, bf16[2,72,384]{2,1,0:T(8,128)(2,1)S(1)}, u32[]{:S(2)}, u32[]{:S(2)}) collective-permute-start(bf16[2,72,384]{2,1,0:T(8,128)(2,1)S(1)} %get-tuple-element.107), channel_id=1, source_target_pairs={{0,4},{1,5},{2,6},{3,7},{4,8},{5,9},{6,10},{7,11},{8,12},{9,13},{1... | collective-permute-start | bytes 331784 | tf_op jit(solution)/shard_map/ppermute | solution.py:601
  728.7 10.0 %collective-permute-start.18 = (bf16[2,72,384]{2,1,0:T(8,128)(2,1)S(1)}, bf16[2,72,384]{2,1,0:T(8,128)(2,1)S(1)}, u32[]{:S(2)}, u32[]{:S(2)}) collective-permute-start(bf16[2,72,384]{2,1,0:T(8,128)(2,1)S(1)} %get-tuple-element.108), channel_id=1, source_target_pairs={{0,12},{1,13},{2,14},{3,15},{4,0},{5,1},{6,2},{7,3},{8,4},{9,5},{1... | collective-permute-start | bytes 331784 | tf_op jit(solution)/shard_map/ppermute | solution.py:601
  731.5 17.9 %collective-permute-start.17 = (bf16[2,72,384]{2,1,0:T(8,128)(2,1)S(1)}, bf16[2,72,384]{2,1,0:T(8,128)(2,1)S(1)}, u32[]{:S(2)}, u32[]{:S(2)}) collective-permute-start(bf16[2,72,384]{2,1,0:T(8,128)(2,1)S(1)} %get-tuple-element.109), channel_id=1, source_target_pairs={{0,8},{1,9},{2,10},{3,11},{4,12},{5,13},{6,14},{7,15},{8,0},{9,1},... | collective-permute-start | bytes 331784 | tf_op jit(solution)/shard_map/ppermute | solution.py:601
  734.1 15.4 %collective-permute-start.22 = (bf16[6,72,384]{2,1,0:T(8,128)(2,1)S(1)}, bf16[6,72,384]{2,1,0:T(8,128)(2,1)S(1)}, u32[]{:S(2)}, u32[]{:S(2)}) collective-permute-start(bf16[6,72,384]{2,1,0:T(8,128)(2,1)S(1)} %get-tuple-element.104), channel_id=1, source_target_pairs={{0,4},{1,5},{2,6},{3,7},{4,8},{5,9},{6,10},{7,11},{8,12},{9,13},{1... | collective-permute-start | bytes 995336 | tf_op jit(solution)/shard_map/ppermute | solution.py:601
  736.2 18.4 %collective-permute-start.24 = (bf16[6,72,384]{2,1,0:T(8,128)(2,1)S(1)}, bf16[6,72,384]{2,1,0:T(8,128)(2,1)S(1)}, u32[]{:S(2)}, u32[]{:S(2)}) collective-permute-start(bf16[6,72,384]{2,1,0:T(8,128)(2,1)S(1)} %get-tuple-element.105), channel_id=1, source_target_pairs={{0,12},{1,13},{2,14},{3,15},{4,0},{5,1},{6,2},{7,3},{8,4},{9,5},{1... | collective-permute-start | bytes 995336 | tf_op jit(solution)/shard_map/ppermute | solution.py:601
  738.0 32.7 %collective-permute-start.23 = (bf16[6,72,384]{2,1,0:T(8,128)(2,1)S(1)}, bf16[6,72,384]{2,1,0:T(8,128)(2,1)S(1)}, u32[]{:S(2)}, u32[]{:S(2)}) collective-permute-start(bf16[6,72,384]{2,1,0:T(8,128)(2,1)S(1)} %get-tuple-element.106), channel_id=1, source_target_pairs={{0,8},{1,9},{2,10},{3,11},{4,12},{5,13},{6,14},{7,15},{8,0},{9,1},... | collective-permute-start | bytes 995336 | tf_op jit(solution)/shard_map/ppermute | solution.py:601
  775.0 27.4 %all-to-all-start = ((bf16[16,80,384]{2,1,0:T(8,128)(2,1)}), bf16[16,80,384]{2,1,0:T(8,128)(2,1)S(1)}, u32[]{:S(2)}, u32[]{:S(2)}) async-start(bf16[16,80,384]{2,1,0:T(8,128)(2,1)} %pad_maximum_fusion.1), calls=%async_computation | async-start | bytes 1966080 | tf_op jit(solution)/shard_map/all_to_all | solution.py:669
  802.4 22.2 %collective-permute-start.25 = (bf16[16,80,384]{2,1,0:T(8,128)(2,1)S(1)}, bf16[16,80,384]{2,1,0:T(8,128)(2,1)S(1)}, u32[]{:S(2)}, u32[]{:S(2)}) collective-permute-start(bf16[16,80,384]{2,1,0:T(8,128)(2,1)S(1)} %all-to-all-done), channel_id=1, source_target_pairs={{0,16},{16,0},{1,17},{17,1},{2,18},{18,2},{3,19},{19,3},{4,20},{20... | collective-permute-start | bytes 2949128 | tf_op jit(solution)/shard_map/ppermute | solution.py:670
  (29 other events, 527.1 us)

commit v3 on v2

--- a/solution.py
+++ b/solution.py
@@ -11,6 +11,7 @@
 FIRST = (((0,), (0,)), ((), ()))
 PLAIN = (((1,), (0,)), ((), ()))
 MASKED = -1e9
+SHORT = pl.CostEstimate(flops=1000, bytes_accessed=1000, transcendentals=0)
 
 
 def mm(left, right, dims):
@@ -71,7 +72,7 @@
                   cos_ref, sin_ref, qm_ref, km_ref, *rest):
     if blocks:
         mine, other = rest[0:3], rest[3:6]
-        n1_ref, q_ref, k_ref, v_ref, attn_ref, stat_ref, w_ref, n1_s, w_s, near, far = rest[6:]
+        n1_ref, q_ref, k_ref, v_ref, attn_ref, stat_ref, w_ref, n1_s, w_s, near, far, back = rest[6:]
     else:
         w_ref, n1_ref, q_ref, k_ref, v_ref, attn_ref, stat_ref, n1_s, w_s, near = rest
     count, width = x_ref.shape
@@ -83,30 +84,38 @@
             core = core_ref[0]
             rows = w_ref.shape[0] // blocks
 
-            def start(block, target, sem):
+            def start(block, sem):
                 for side in (0, 1):
                     def dst(offset, size):
                         base = block * rows + side * (rows // 2) + offset
-                        return target.at[pl.ds(pl.multiple_of(base, 16), size)]
+                        return w_s.at[pl.ds(pl.multiple_of(base, 16), size)]
                     place_pieces(core, slot_ref, mine, other, block, side, dst, sem)
 
             def near_block(block, carry):
-                start(block, w_s, near)
+                start(block, near)
                 return carry
 
             def far_block(block, carry):
-                start(block, w_ref, far)
+                start(block, far)
                 return carry
 
-            lax.fori_loop(0, w_s.shape[0] // rows, near_block, 0)
-            lax.fori_loop(0, blocks, far_block, 0)
+            lax.fori_loop(0, 3 * width // rows, near_block, 0)
+            lax.fori_loop(3 * width // rows, blocks, far_block, 0)
         else:
             pltpu.make_async_copy(w_ref.at[pl.ds(0, 3 * width)], w_s, near).start()
         unit, _ = norm_parts(x_ref[...].astype(F32))
         n1 = (unit * g_ref[...] + b_ref[...]).astype(BF16)
         n1_s[...] = n1
         n1_ref[...] = n1
-        pltpu.make_async_copy(w_s, w_s, near).wait()
+        head = w_s.at[pl.ds(0, 3 * width)]
+        pltpu.make_async_copy(head, head, near).wait()
+
+    if blocks:
+        @pl.when(step == 1)
+        def _():
+            tail = w_s.at[pl.ds(3 * width, w_s.shape[0] - 3 * width)]
+            pltpu.make_async_copy(tail, tail, far).wait()
+            pltpu.make_async_copy(w_s, w_ref, back).start()
 
     def third(j):
         return w_s[pl.ds(pl.multiple_of(j * width + step * 128, 128), 128), :]
@@ -150,7 +159,7 @@
     if blocks:
         @pl.when(step == pl.num_programs(0) - 1)
         def _():
-            pltpu.make_async_copy(w_ref, w_ref, far).wait()
+            pltpu.make_async_copy(w_s, w_ref, back).wait()
 
 
 def attend(core, slots, x, gain, shift, bqkv, cos, sin, qm, km, weights, stack):
@@ -178,11 +187,11 @@
     outs = [pl.BlockSpec((count, width), whole)] + [pl.BlockSpec((count, 128), col)] * 5
     shape = lambda d: jax.ShapeDtypeStruct((count, width), d)
     shapes = [shape(BF16)] * 5 + [shape(F32)]
-    scratch = [pltpu.VMEM((count, width), BF16), pltpu.VMEM((3 * width, width), BF16), pltpu.SemaphoreType.DMA]
+    scratch = [pltpu.VMEM((count, width), BF16), pltpu.VMEM((stack if pieces else 3 * width, width), BF16), pltpu.SemaphoreType.DMA]
     if pieces:
         outs.append(hbm)
         shapes.append(jax.ShapeDtypeStruct((stack, width), BF16))
-        scratch.append(pltpu.SemaphoreType.DMA)
+        scratch += [pltpu.SemaphoreType.DMA] * 2
     return pl.pallas_call(
         functools.partial(attend_kernel, blocks),
         grid=(pairs,),
@@ -191,7 +200,7 @@
         out_shape=shapes,
         scratch_shapes=scratch,
         compiler_params=pltpu.CompilerParams(vmem_limit_bytes=56 * 2**20),
-        cost_estimate=pl.CostEstimate(flops=30 * 10**9, bytes_accessed=40 * 10**6, transcendentals=0),
+        cost_estimate=SHORT,
         name="attend",
     )(core, slots, x, gain, shift, bqkv, bqkv, bqkv, cos, sin, qm, km, *given)
 
@@ -349,30 +358,15 @@
             pltpu.SemaphoreType.DMA((3,)),
         ],
         compiler_params=pltpu.CompilerParams(vmem_limit_bytes=60 * 2**20),
-        cost_estimate=pl.CostEstimate(flops=60 * 10**9, bytes_accessed=50 * 10**6, transcendentals=0),
+        cost_estimate=SHORT,
         name="mlp",
     )(core, x, attn, cot, live, vectors, weights, weights, weights, b1)
 
 
-def back_kernel(block_rows, start, first, final, core_ref, q_ref, k_ref, v_ref, da_ref, at_ref, stat_ref, cos_ref, sin_ref,
-                qm_ref, km_ref, pos_ref, n1_ref, wq_ref, wk_ref, wv_ref, *rest):
-    if not first:
-        before_ref, rest = rest[0], rest[3:]
-    if final:
-        x_ref, dm_ref, vec_ref = rest[:3]
-        rest = rest[3:]
-        gb_ref, gf_ref, ig_ref, ln_ref, keep_ref, give_ref, dn_ref, stage_s, sems = rest
-    else:
-        gb_ref, gf_ref, dn_ref, keep_ref, give_ref, stage_s, sems = rest
+def back_kernel(first, q_ref, k_ref, v_ref, da_ref, at_ref, stat_ref, cos_ref, sin_ref,
+                qm_ref, km_ref, pos_ref, *rest):
+    dq_ref, dk_ref, dv_ref, gb_ref, gf_ref = rest if first else rest[5:]
     count = q_ref.shape[0]
-    width = n1_ref.shape[1]
-    step = pl.program_id(0)
-    core = core_ref[0]
-
-    @pl.when(step == 0)
-    def _():
-        dn_ref[...] = jnp.zeros_like(dn_ref) if first else before_ref[...]
-
     lane = lax.broadcasted_iota(jnp.int32, (1, 128), 1)
     zero = jnp.zeros((), BF16)
     q = q_ref[...]
@@ -425,96 +419,128 @@
     dvp = dv.astype(BF16)
     gb_ref[...] = jnp.concatenate(
         [row(dqp.astype(F32)), row(dkp.astype(F32)), row(dvp.astype(F32)), jnp.zeros((5, 128), F32)], axis=0)
-    d = jnp.concatenate([dqp, dkp, dvp], axis=1)
-    w = jnp.concatenate([wq_ref[...], wk_ref[...], wv_ref[...]], axis=0)
-    dn_ref[...] += mm(d, w, PLAIN)
-    slot = lax.rem(step, 2)
-
-    @pl.when(step >= 2)
-    def _():
-        pltpu.make_async_copy(stage_s.at[slot], stage_s.at[slot], sems.at[slot]).wait()
-
-    stage_s[slot] = mm(d, n1_ref[...], FIRST).astype(BF16)
-    for j in range(3):
-        send_rows(core, block_rows, stage_s.at[slot, pl.ds(128 * j, 128)], j * width + (start + step) * 128,
-                  0, keep_ref, give_ref, sems.at[slot])
+    dq_ref[...] = dqp
+    dk_ref[...] = dkp
+    dv_ref[...] = dvp
+
+
+def attend_back(start, stop, before, q, k, v, da, attn, stat, cos, sin, qm, km, pos):
+    count, width = q.shape
+    whole = lambda p: (0, 0)
+    col = lambda p: (0, p + start)
+    tall = pl.BlockSpec((count, 128), col)
+    fixed = pl.BlockSpec((count, 128), whole)
+    small = pl.BlockSpec((8, 128), col)
+    in_specs = [tall] * 8 + [fixed] * 2 + [pl.BlockSpec((count, 2), whole)]
+    operands = [q, k, v, da, attn, stat, cos, sin, qm, km, pos]
+    aliases = {}
+    if before is not None:
+        aliases = {len(operands) + i: i for i in range(5)}
+        in_specs += [pl.BlockSpec(memory_space=pl.ANY)] * 5
+        operands += list(before)
+    return pl.pallas_call(
+        functools.partial(back_kernel, before is None),
+        grid=(stop - start,),
+        in_specs=in_specs,
+        out_specs=[tall] * 3 + [small] * 2,
+        out_shape=[jax.ShapeDtypeStruct((count, width), BF16)] * 3 + [jax.ShapeDtypeStruct((8, width), F32)] * 2,
+        input_output_aliases=aliases,
+        compiler_params=pltpu.CompilerParams(vmem_limit_bytes=56 * 2**20),
+        cost_estimate=SHORT,
+        name="attend_back",
+    )(*operands)
+
+
+def qkv_grad_kernel(block_rows, core_ref, dq_ref, dk_ref, dv_ref, n1_ref, keep_ref, give_ref, stage_s, sem):
+    width = n1_ref.shape[1]
+    cols = dq_ref.shape[1]
+    step = pl.program_id(0)
+    n1 = n1_ref[...]
+    for j, ref in enumerate((dq_ref, dk_ref, dv_ref)):
+        stage_s[step, j] = mm(ref[...], n1, FIRST).astype(BF16)
+        send_rows(core_ref[0], block_rows, stage_s.at[step, j], j * width + step * cols, 0, keep_ref, give_ref, sem)
 
     @pl.when(step == pl.num_programs(0) - 1)
     def _():
-        pltpu.make_async_copy(stage_s.at[slot], stage_s.at[slot], sems.at[slot]).wait()
-        pltpu.make_async_copy(stage_s.at[1 - slot], stage_s.at[1 - slot], sems.at[1 - slot]).wait()
-        if final:
-            unit, inverse = norm_parts(x_ref[...].astype(F32))
-            dn = dn_ref[...]
-            ig_ref[...] = dm_ref[...] + norm_back(unit, inverse, dn, vec_ref[0:1, :])
-            ln_ref[...] = jnp.concatenate([row(dn * unit), row(dn), jnp.zeros((6, width), F32)], axis=0)
-
-
-def attend_back(core, start, stop, before, final, q, k, v, da, attn, stat, cos, sin, qm, km, pos, n1, weights, block_rows):
-    count, width = q.shape
-    pairs = width // 128
-    whole = lambda p: (0, 0)
-    col = lambda p: (0, p + start)
-    big = pl.BlockSpec((count, width), whole)
-    tall = pl.BlockSpec((count, 128), col)
-    fixed = pl.BlockSpec((count, 128), whole)
+        pltpu.make_async_copy(stage_s, stage_s, sem).wait()
+
+
+def qkv_grad(core, dq, dk, dv, n1, block_rows):
+    count, width = n1.shape
+    cols = width // 2
+    tall = pl.BlockSpec((count, cols), lambda p: (0, p))
     hbm = pl.BlockSpec(memory_space=pl.ANY)
-    w = [pl.BlockSpec((128, width), lambda p, j=j: (p + start + j * pairs, 0)) for j in range(3)]
-    small = pl.BlockSpec((8, 128), lambda p: (0, p))
-    in_specs = ([pl.BlockSpec(memory_space=pltpu.SMEM)] + [tall] * 8 + [fixed] * 2
-                + [pl.BlockSpec((count, 2), whole), big] + w)
-    operands = [core, q, k, v, da, attn, stat, cos, sin, qm, km, pos, n1, weights, weights, weights]
-    out_specs = [small] * 2
-    out_shape = [jax.ShapeDtypeStruct((8, 128 * (stop - start)), F32)] * 2
-    dn_shape = jax.ShapeDtypeStruct((count, width), F32)
-    scratch = [pltpu.VMEM((2, 384, width), BF16), pltpu.SemaphoreType.DMA((2,))]
-    aliases = {}
-    if before is not None:
-        aliases = {len(operands) + 1: 4 if final else 3, len(operands) + 2: 5 if final else 4}
-        in_specs += [big, hbm, hbm]
-        operands += list(before)
-    if final is not None:
-        in_specs += [big, big, pl.BlockSpec(final[2].shape, whole)]
-        operands += list(final)
-        out_specs += [big, pl.BlockSpec((8, width), whole), hbm, hbm]
-        out_shape += [dn_shape, jax.ShapeDtypeStruct((8, width), F32)] + grad_shapes(block_rows, 3 * width, width)
-        scratch = [pltpu.VMEM((count, width), F32)] + scratch
-    else:
-        out_specs += [big, hbm, hbm]
-        out_shape += [dn_shape] + grad_shapes(block_rows, 3 * width, width)
     return pl.pallas_call(
-        functools.partial(back_kernel, block_rows, start, before is None, final is not None),
-        grid=(stop - start,),
-        in_specs=in_specs,
-        out_specs=out_specs,
-        out_shape=out_shape,
-        scratch_shapes=scratch,
-        input_output_aliases=aliases,
-        compiler_params=pltpu.CompilerParams(vmem_limit_bytes=60 * 2**20),
-        cost_estimate=pl.CostEstimate(flops=10 * 10**9 * (stop - start), bytes_accessed=30 * 10**6, transcendentals=0),
-        name="attend_back",
-    )(*operands)
-
-
-def fold_kernel(pos_ref, *refs):
-    keep, got, send_ref, hold_ref = refs[:4], refs[4:8], refs[8], refs[9]
-    for k in range(4):
-        out = (send_ref, hold_ref)[k // 2]
-        out[k % 2, 0] = (keep[k][0].astype(F32) + got[k][0].astype(F32)).astype(BF16)
-
-
-def fold(pos, keep, got):
+        functools.partial(qkv_grad_kernel, block_rows),
+        grid=(2,),
+        in_specs=[pl.BlockSpec(memory_space=pltpu.SMEM)] + [tall] * 3 + [pl.BlockSpec((count, width), lambda p: (0, 0))],
+        out_specs=[hbm, hbm],
+        out_shape=grad_shapes(block_rows, 3 * width, width),
+        scratch_shapes=[pltpu.VMEM((2, 3, cols, width), BF16), pltpu.SemaphoreType.DMA],
+        compiler_params=pltpu.CompilerParams(vmem_limit_bytes=56 * 2**20),
+        cost_estimate=SHORT,
+        name="qkv_grad",
+    )(core, dq, dk, dv, n1)
+
+
+def input_kernel(dq_ref, dk_ref, dv_ref, w_ref, x_ref, dm_ref, vec_ref, ig_ref, ln_ref):
+    d = jnp.concatenate([dq_ref[...], dk_ref[...], dv_ref[...]], axis=1)
+    dn = mm(d, w_ref[...], PLAIN)
+    unit, inverse = norm_parts(x_ref[...].astype(F32))
+    ig_ref[...] = dm_ref[...] + norm_back(unit, inverse, dn, vec_ref[0:1, :])
+    row = lambda a: jnp.sum(a, axis=0, keepdims=True)
+    sums = jnp.concatenate([row(dn * unit), row(dn), jnp.zeros((6, dn.shape[1]), F32)], axis=0)
+
+    @pl.when(pl.program_id(0) == 0)
+    def _():
+        ln_ref[...] = sums
+
+    @pl.when(pl.program_id(0) > 0)
+    def _():
+        ln_ref[...] += sums
+
+
+def input_back(dq, dk, dv, weights, x, dm, vectors):
+    count, width = x.shape
+    tile = 256
+    part = pl.BlockSpec((tile, width), lambda i: (i, 0))
+    whole = lambda i: (0, 0)
+    return pl.pallas_call(
+        input_kernel,
+        grid=(count // tile,),
+        in_specs=[part] * 3 + [pl.BlockSpec((3 * width, width), whole), part, part, pl.BlockSpec(vectors.shape, whole)],
+        out_specs=[part, pl.BlockSpec((8, width), whole)],
+        out_shape=[jax.ShapeDtypeStruct((count, width), F32), jax.ShapeDtypeStruct((8, width), F32)],
+        compiler_params=pltpu.CompilerParams(vmem_limit_bytes=56 * 2**20),
+        cost_estimate=SHORT,
+        name="input_back",
+    )(dq, dk, dv, weights, x, dm, vectors)
+
+
+def fold_kernel(count, pos_ref, *refs):
+    out_ref = refs[-1]
+    ways = out_ref.shape[0]
+    for k in range(ways):
+        total = refs[k][0].astype(F32) + refs[ways + k][0].astype(F32)
+        for more in refs[2 * ways:-1]:
+            total = total + more[0, 0].astype(F32)
+        out_ref[k, 0] = total.astype(BF16)
+
+
+def fold(pos, keep, got, ways, more=()):
     count, rows, width = keep.shape
-    quarter = [pl.BlockSpec((1, rows // 2, width // 2), lambda i, pos, k=k: (i, pos[k, 0], pos[k, 1])) for k in range(4)]
-    out = pl.BlockSpec((2, 1, rows // 2, width // 2), lambda i, pos: (0, i, 0, 0))
-    shape = jax.ShapeDtypeStruct((2, count, rows // 2, width // 2), BF16)
+    quarter = [pl.BlockSpec((1, rows // 2, width // 2), lambda i, pos, k=k: (i, pos[k, 0], pos[k, 1])) for k in ways]
+    extra = [pl.BlockSpec((1, 1, rows // 2, width // 2), lambda i, pos, at=at: (at, i, 0, 0)) for _, at in more]
+    out = pl.BlockSpec((len(ways), 1, rows // 2, width // 2), lambda i, pos: (0, i, 0, 0))
+    shape = jax.ShapeDtypeStruct((len(ways), count, rows // 2, width // 2), BF16)
     return pl.pallas_call(
-        fold_kernel,
+        functools.partial(fold_kernel, len(more)),
         grid_spec=pltpu.PrefetchScalarGridSpec(
-            num_scalar_prefetch=1, grid=(count,), in_specs=quarter * 2, out_specs=[out, out]),
-        out_shape=[shape, shape],
+            num_scalar_prefetch=1, grid=(count,), in_specs=quarter * 2 + extra, out_specs=out),
+        out_shape=shape,
+        cost_estimate=SHORT,
         name="fold",
-    )(pos, *([keep] * 4), *([got] * 4))
+    )(pos, *([keep] * len(ways)), *([got] * len(ways)), *[a for a, _ in more])
 
 
 def adam_kernel(scal_ref, a_ref, b_ref, w_ref, m_ref, v_ref, g_out, v_out, w_out):
@@ -631,30 +657,28 @@
     return (first, second, small, *other), slots, tables
 
 
-def reduce_blocks(keep, give, core, me, devices):
-    count, rows, width = keep.shape
-    x, y, z = me & 1, (me >> 1) & 1, me // 4
+def quarters(core, me):
+    x, y = me & 1, (me >> 1) & 1
     one = jnp.where(core == 0, x, y)
     two = jnp.where(core == 0, y, x)
     pairs = [(1 - one, 1 - two), (1 - one, two), (one, 1 - two), (one, two)]
-    pos = jnp.stack([
+    return jnp.stack([
         jnp.stack([jnp.where(core == 0, b, a), jnp.where(core == 0, a, b)]) for a, b in pairs
     ]).astype(jnp.int32)
-    got = lax.ppermute(give, "group", SWAP)
-    send, hold = fold(pos, keep, got)
-    came = cross(send, 1, 2, devices)
-
-    def add(a, b):
-        return a.astype(F32) + b.astype(F32)
-
-    again = cross(add(hold[0], came[0]).astype(BF16), 2, 1, devices)
-    total = add(add(hold[1], came[1]), again).reshape(count, 4, rows // 8, width // 2)
-    low = total.astype(BF16)
-    pick = lambda a, at: lax.dynamic_index_in_dim(a, at, 1, keepdims=False)
-    parts = along_z([pick(low, lax.rem(z + s, 4)) for s in (1, 2, 3)], devices)
-    total = pick(total, z)
-    for part in parts:
-        total = add(total, part)
+
+
+def sum_z(low, me, devices):
+    count, rows, cols = low.shape
+    z = me // 4
+    low = low.reshape(count, 4, rows // 4, cols)
+    pick = lambda at: lax.dynamic_index_in_dim(low, at, 1, keepdims=False)
+    return (pick(z), *along_z([pick(lax.rem(z + s, 4)) for s in (1, 2, 3)], devices))
+
+
+def total_of(parts):
+    total = parts[0].astype(F32)
+    for part in parts[1:]:
+        total = total + part.astype(F32)
     return total
 
 
@@ -748,26 +772,45 @@
     block_out, grad_middle, grad_attn, sums, bias_up, keep_mlp, give_mlp = mlp(
         here, x, attn, cotangent[0], alive, vectors, weights, vectors[8:12].reshape(1, 4 * width), whole_rows
     )
+    pairs = width // 128
+    tie = lax.optimization_barrier
     if quick:
-        late = reduce_blocks(keep_mlp, give_mlp, core, me, devices)
-    pairs = width // 128
-    fixed = (query, key, value, grad_attn, attn, stat, cosine, sine, query_mask, key_mask, places, first_in, weights)
-    cut = pairs // 2
-    gb1, gf1, *before = attend_back(here, 0, cut, None, None, *fixed, whole_rows)
-    gb2, gf2, input_grad, norm_sums, keep_qkv, give_qkv = attend_back(
-        here, cut, pairs, before, (x, grad_middle, vectors), *fixed, whole_rows
-    )
-    grad_bias = jnp.concatenate([gb1, gb2], axis=1)
-    grad_freq = jnp.concatenate([gf1, gf2], axis=1)
+        pos = quarters(core, me)
+        got = lax.ppermute(give_mlp, "group", SWAP)
+    back = None
+    cuts = (0, 1, pairs - 2, pairs)
+    for start, stop in zip(cuts[:-1], cuts[1:]):
+        back = attend_back(
+            start, stop, back, query, key, value, grad_attn, attn, stat, cosine, sine, query_mask, key_mask, places
+        )
+        if quick and start == 0:
+            send, back = tie((fold(pos, keep_mlp, got, (0, 1)), back))
+            came = cross(send, 1, 2, devices)
+        if quick and start == 1:
+            send, back = tie((fold(pos, keep_mlp, got, (2,), ((came, 0),)), back))
+            again = cross(send, 2, 1, devices)
+    grad_q, grad_k, grad_v, grad_bias, grad_freq = back
+    if quick:
+        low, grad_q = tie((fold(pos, keep_mlp, got, (3,), ((came, 1), (again, 0)))[0], grad_q))
+        late = sum_z(low, me, devices)
+    keep_qkv, give_qkv = qkv_grad(here, grad_q, grad_k, grad_v, first_in, whole_rows)
+    grad_v, give_qkv = tie((grad_v, give_qkv))
+    input_grad, norm_sums = input_back(grad_q, grad_k, grad_v, weights, x, grad_middle, vectors)
     grad_freqs = grad_freq[:2].reshape(2, heads, 2, half).sum(2).reshape(1, width)
     local_vec = jnp.concatenate(
         [norm_sums[:2], sums[:2], grad_bias[:3], sums[2:3], bias_up.reshape(4, width), sums[3:4], grad_freqs],
         axis=0,
     )
     if quick:
-        early = reduce_blocks(keep_qkv, give_qkv, core, me, devices)
+        got_qkv = lax.ppermute(give_qkv, "group", SWAP)
+        got_qkv, norm_sums = tie((got_qkv, norm_sums))
+        came = cross(fold(pos, keep_qkv, got_qkv, (0, 1)), 1, 2, devices)
+        came, late = tie((came, late))
+        again = cross(fold(pos, keep_qkv, got_qkv, (2,), ((came, 0),)), 2, 1, devices)
+        early = sum_z(fold(pos, keep_qkv, got_qkv, (3,), ((came, 1), (again, 0)))[0], me, devices)
+        early, late = total_of(early), total_of(late)
         vec_total = sum_everywhere(local_vec + lax.ppermute(local_vec, "group", SWAP), devices)
-        total = jnp.concatenate([early, late])
+        total, vec_total = lax.optimization_barrier((jnp.concatenate([early, late]), vec_total))
         mine, other, square = share_blocks(total, owner_block, core, devices)
     else:
         vec_total = lax.psum(local_vec, CORES)

time: 845 us -> 449 us (0.53)
  Pallas kernels: 591 us -> 213 us
  waiting for transfers between devices: 138 us -> 101 us
  blocking collectives: 0 us -> 24.8 us
    pallas_call x1, Pallas kernels: 434 us -> 31.8 us  [attend(): pl.pallas_call(functools.partial(attend_kernel, blocks), grid=(pairs,), i...]
    all_to_all x0 -> x1, blocking collectives: none -> 24.8 us  [share_blocks(): mine = lax.all_to_all(load, 'dp', 0, 0, tiled=True)]
    all_to_all x1 -> x0, waiting for transfers between devices: 21.4 us -> none  [share_blocks(): mine = lax.all_to_all(load, 'dp', 0, 0, tiled=True)]
    ppermute x8, waiting for transfers between devices: 69.8 us -> 53.4 us  [cross(): return lax.ppermute(value, CORES, perm)]
    pallas_call x4 -> x11, Pallas kernels: 81.7 us -> 97.2 us  [the longest x3 49.7 us: attend_back(): pl.pallas_call(functools.partial(back_kernel, before is None), grid=(stop...]
    pallas_call x1, Pallas kernels: 68.6 us -> 78.3 us  [mlp(): pl.pallas_call(functools.partial(mlp_kernel, block_rows, base), grid=(uni...]
  transfers between devices with their start and end apart: 32 -> 31, of which waited for: 17 -> 16; matrix products, arithmetic and copies ran while one was open for 4% -> 7% of each run, Pallas kernels for 9% -> 14%
where the time goes in v3:
time: 449 us; the launch traced here: 440 us
  Pallas kernels  213 us (47%)
  waiting for transfers between devices  101 us (22%)
  starting transfers between devices  47.7 us (11%)
  other arithmetic  26.5 us (6%)
  blocking collectives  24.8 us (6%)
  local copies, waits for them, and re-layouts  18.9 us (4%)
  between operations  7.99 us (2%)
    pallas_call x1, Pallas kernels, mlp(): pl.pallas_call(functools.partial(mlp_kernel, block_rows, base), grid=(uni...  78.3 us
    ppermute x8, waiting for transfers between devices, cross(): return lax.ppermute(value, CORES, perm)  53.4 us
    pallas_call x3, Pallas kernels, attend_back(): pl.pallas_call(functools.partial(back_kernel, before is None), grid=(stop...  49.7 us
    ppermute x12, waiting for transfers between devices, along_z(): lax.ppermute(v, 'dp', [(i, (i + 4 * (s + 1)) % devices) for i in range(de...  33 us
    pallas_call x1, Pallas kernels, attend(): pl.pallas_call(functools.partial(attend_kernel, blocks), grid=(pairs,), i...  31.8 us
    ppermute x12, starting transfers between devices, along_z(): lax.ppermute(v, 'dp', [(i, (i + 4 * (s + 1)) % devices) for i in range(de...  30.2 us
    pallas_call x6, Pallas kernels, fold(): pl.pallas_call(functools.partial(fold_kernel, len(more)), grid_spec=pltpu...  28.2 us
    all_to_all x1, blocking collectives, share_blocks(): mine = lax.all_to_all(load, 'dp', 0, 0, tiled=True)  24.8 us
  transfers between devices with their start and end apart: 31, of which 16 were waited for; matrix products, arithmetic and copies ran while one was open for 7% of the time, Pallas kernels for 14%

profile of v3, /device:TPU:0, one launch (start us, length us, event | category | flops | bytes accessed | tf_op | source)
XLA Modules:
  0.0 440.1 jit_solution(9745874274210416279)
XLA Ops:
  2.0 4.1 collective-permute-start.1
  13.5 13.0 %negate_select_fusion = (f32[1024,768]{1,0:T(8,128)}, f32[1024,768]{1,0:T(8,128)}) fusion(f32[768]{0:T(1024)S(1)} %mul.147, f32[1024]{0:T(1024)S(1)} %get-tuple-element.180, f32[768]{0:T(1024)S(1)} %mul.143, f32[1024]{0:T(1024)S(1)} %get-tuple-element.179, pred[768]{0:T(1024)(128)(4,1)S(1)} %fusion.17), kind=kLoop, calls=%fused_computation.1 | loop fusion | flops 3932160 | bytes 6306560 | tf_op jit(solution)/shard_map/jit(_where)/select_n | solution.py:748
  35.8 16.8 %collective-permute-done.5 = bf16[4,208,768]{2,1,0:T(8,128)(2,1)S(1)} collective-permute-done((bf16[4,208,768]{2,1,0:T(8,128)(2,1)S(1)}, bf16[4,208,768]{2,1,0:T(8,128)(2,1)S(1)}, u32[]{:S(2)}, u32[]{:S(2)}) %collective-permute-start.5) | collective-permute-done | bytes 1277984 | tf_op jit(solution)/shard_map/ppermute | solution.py:622
  56.0 3.8 collective-permute-start.9
  59.9 25.2 %collective-permute-done.6.rest_1_ = bf16[8,208,768]{2,1,0:T(8,128)(2,1)} collective-permute-done((bf16[8,208,768]{2,1,0:T(8,128)(2,1)S(1)}, bf16[8,208,768]{2,1,0:T(8,128)(2,1)}, u32[]{:S(2)}, u32[]{:S(2)}) %collective-permute-start.6) | collective-permute-done | bytes 2555936 | tf_op jit(solution)/shard_map/ppermute | solution.py:622
  93.0 31.8 %attend.1 = (bf16[1024,768]{1,0:T(8,128)(2,1)}, bf16[1024,768]{1,0:T(8,128)(2,1)}, bf16[1024,768]{1,0:T(8,128)(2,1)}, bf16[1024,768]{1,0:T(8,128)(2,1)}, bf16[10...) custom-call(s32[1]{0:T(128)} %bitcast.core_ref, s32[4,16]{1,0:T(4,128)} %pad_add_fusion.1.slot_ref, ...), custom_call_target="tpu_custom_call" | custom-call | flops 1000 | bytes 1000 | tf_op jit(solution)/shard_map/attend/pallas_call | solution.py:195
  124.8 78.3 %mlp.1 = (bf16[1024,768]{1,0:T(8,128)(2,1)}, f32[1024,768]{1,0:T(8,128)}, bf16[1024,768]{1,0:T(8,128)(2,1)}, f32[8,768]{1,0:T(8,128)}, f32[1,3072]{1,0:T(1,128)}...) custom-call(s32[1]{0:T(128)} %bitcast.core_ref, bf16[1024,768]{1,0:T(8,128)(2,1)} %bitcast.83, ...), custom_call_target="tpu_custom_call" | custom-call | flops 1000 | bytes 1000 | tf_op jit(solution)/shard_map/mlp/pallas_call | solution.py:334
  204.1 9.6 %attend_back.3 = (bf16[1024,768]{1,0:T(8,128)(2,1)}, bf16[1024,768]{1,0:T(8,128)(2,1)}, bf16[1024,768]{1,0:T(8,128)(2,1)}, f32[8,768]{1,0:T(8,128)}, f32[8,768]{1,0:T(8,128)}) custom-call(bf16[1024,768]{1,0:T(8,128)(2,1)} %get-tuple-element.91.q_ref, bf16[1024,768]{1,0:T(8,128)(2,1)} %get-tuple-element.92.k_ref, bf16[1024,768]{1,0:T(8,128)(2,1)} %get-tuple-element.93.v_ref, ...), custom_call_target="tpu_custom_call" | custom-call | flops 1000 | bytes 1000 | tf_op jit(solution)/shard_map/attend_back/pallas_call | solution.py:441
  213.7 6.6 %fold.6 = bf16[2,6,288,384]{3,2,1,0:T(8,128)(2,1)} custom-call(s32[4,2]{1,0:T(4,128)} %pad_add_fusion.2.pos_ref, bf16[6,576,768]{2,1,0:T(8,128)(2,1)} %get-tuple-element.89.refs_0_.refs_1_, bf16[6,576,768]{2,1,0:T(8,128)(2,1)} %get-tuple-element.89.refs_0_.refs_1_, bf16[6,576,768]{2,1,0:T(8,128)(2,1)} %collective-permute-done.13.refs_2_.refs_3_.refs_1_, ...), custom_call_target="tpu_custom_call" | custom-call | flops 1000 | bytes 1000 | tf_op jit(solution)/shard_map/fold/pallas_call | solution.py:536
  220.8 23.3 %attend_back.4 = (bf16[1024,768]{1,0:T(8,128)(2,1)}, bf16[1024,768]{1,0:T(8,128)(2,1)}, bf16[1024,768]{1,0:T(8,128)(2,1)}, f32[8,768]{1,0:T(8,128)}, f32[8,768]{1,0:T(8,128)}) custom-call(bf16[1024,768]{1,0:T(8,128)(2,1)} %get-tuple-element.91.q_ref, ...), custom_call_target="tpu_custom_call", output_to_operand_aliasing={{0}: (11, {}), {1}: (12, {}), {2}: (13, {}), {3}: (14, {}),... | custom-call | flops 1000 | bytes 1000 | tf_op jit(solution)/shard_map/attend_back/pallas_call | solution.py:441
  244.1 8.4 %collective-permute-done.14.refs_2_ = bf16[2,6,288,384]{3,2,1,0:T(8,128)(2,1)S(1)} collective-permute-done((bf16[2,6,288,384]{3,2,1,0:T(8,128)(2,1)}, bf16[2,6,288,384]{3,2,1,0:T(8,128)(2,1)S(1)}, u32[]{:S(2)}, u32[]{:S(2)}) %collective-permute-start.14) | collective-permute-done | bytes 2654240 | tf_op jit(solution)/shard_map/ppermute | solution.py:622
  254.1 5.8 %fold.7 = bf16[1,6,288,384]{3,2,1,0:T(8,128)(2,1)} custom-call(s32[4,2]{1,0:T(4,128)} %pad_add_fusion.2.pos_ref, bf16[6,576,768]{2,1,0:T(8,128)(2,1)} %get-tuple-element.89.refs_0_.refs_1_, bf16[6,576,768]{2,1,0:T(8,128)(2,1)} %collective-permute-done.13.refs_2_.refs_3_.refs_1_, bf16[2,6,288,384]{3,2,1,0:T(8,128)(2,1)} %copy-done.1), custom_call_target="tpu_custom_call" | custom-call | flops 1000 | bytes 1000 | tf_op jit(solution)/shard_map/fold/pallas_call | solution.py:536
  261.9 16.8 %attend_back.5 = (bf16[1024,768]{1,0:T(8,128)(2,1)}, bf16[1024,768]{1,0:T(8,128)(2,1)}, bf16[1024,768]{1,0:T(8,128)(2,1)}, f32[8,768]{1,0:T(8,128)}, f32[8,768]{1,0:T(8,128)}) custom-call(bf16[1024,768]{1,0:T(8,128)(2,1)} %get-tuple-element.91.q_ref, ...), custom_call_target="tpu_custom_call", output_to_operand_aliasing={{0}: (11, {}), {1}: (12, {}), {2}: (13, {}), {3}: (14, {}),... | custom-call | flops 1000 | bytes 1000 | tf_op jit(solution)/shard_map/attend_back/pallas_call | solution.py:441
  279.8 6.2 %fold.8 = bf16[1,6,288,384]{3,2,1,0:T(8,128)(2,1)} custom-call(s32[4,2]{1,0:T(4,128)} %pad_add_fusion.2.pos_ref, bf16[6,576,768]{2,1,0:T(8,128)(2,1)} %get-tuple-element.89.refs_0_.refs_1_, bf16[6,576,768]{2,1,0:T(8,128)(2,1)} %collective-permute-done.13.refs_2_.refs_3_.refs_1_, bf16[2,6,288,384]{3,2,1,0:T(8,128)(2,1)} %copy-done.1, ...), custom_call_target="tpu_custom_call" | custom-call | flops 1000 | bytes 1000 | tf_op jit(solution)/shard_map/fold/pallas_call | solution.py:536
  286.1 9.2 %qkv_grad.1 = (bf16[2,576,768]{2,1,0:T(8,128)(2,1)}, bf16[2,576,768]{2,1,0:T(8,128)(2,1)}) custom-call(s32[1]{0:T(128)} %bitcast.core_ref, bf16[1024,768]{1,0:T(8,128)(2,1)} %get-tuple-element.120.dq_ref, bf16[1024,768]{1,0:T(8,128)(2,1)} %get-tuple-element.121.dk_ref, bf16[1024,768]{1,0:T(8,128)(2,1)} %get-tuple-element.125.dv_ref, ...), custom_call_target="tpu_custom_call" | custom-call | flops 1000 | bytes 1000 | tf_op jit(solution)/shard_map/qkv_grad/pallas_call | solution.py:473
  295.4 10.0 %input_back.1 = (f32[1024,768]{1,0:T(8,128)}, f32[8,768]{1,0:T(8,128)}) custom-call(bf16[1024,768]{1,0:T(8,128)(2,1)} %get-tuple-element.120.dq_ref, bf16[1024,768]{1,0:T(8,128)(2,1)} %get-tuple-element.121.dk_ref, bf16[1024,768]{1,0:T(8,128)(2,1)} %get-tuple-element.125.dv_ref, bf16[9216,768]{1,0:T(8,128)(2,1)} %get-tuple-element.87.wo_ref.w1_ref.w2_ref.w_ref, ...), custom_call_target="tpu_custom_call" | custom-call | flops 1000 | bytes 1000 | tf_op jit(solution)/shard_map/input_back/pallas_call | solution.py:508
  310.9 13.4 %collective-permute-start.20 = (bf16[6,72,384]{2,1,0:T(8,128)(2,1)}, bf16[6,72,384]{2,1,0:T(8,128)(2,1)S(1)}, u32[]{:S(2)}, u32[]{:S(2)}) collective-permute-start(bf16[6,72,384]{2,1,0:T(8,128)(2,1)} %get-tuple-element.158), channel_id=1, source_target_pairs={{0,12},{1,13},{2,14},{3,15},{4,0},{5,1},{6,2},{7,3},{8,4},{9,5},{1... | collective-permute-start | bytes 995336 | tf_op jit(solution)/shard_map/ppermute | solution.py:627
  326.1 6.8 %collective-permute-done.20 = bf16[6,72,384]{2,1,0:T(8,128)(2,1)S(1)} collective-permute-done((bf16[6,72,384]{2,1,0:T(8,128)(2,1)}, bf16[6,72,384]{2,1,0:T(8,128)(2,1)S(1)}, u32[]{:S(2)}, u32[]{:S(2)}) %collective-permute-start.20) | collective-permute-done | bytes 331808 | tf_op jit(solution)/shard_map/ppermute | solution.py:627
  332.9 20.1 %collective-permute-done.19 = bf16[6,72,384]{2,1,0:T(8,128)(2,1)S(1)} collective-permute-done((bf16[6,72,384]{2,1,0:T(8,128)(2,1)S(1)}, bf16[6,72,384]{2,1,0:T(8,128)(2,1)S(1)}, u32[]{:S(2)}, u32[]{:S(2)}) %collective-permute-start.19) | collective-permute-done | bytes 331808 | tf_op jit(solution)/shard_map/ppermute | solution.py:627
  361.7 4.0 collective-permute-done.26
  374.0 3.7 collective-permute-start.29
  385.4 3.6 collective-permute-start.24
  399.6 24.8 %all_to_all.5 = bf16[16,80,384]{2,1,0:T(8,128)(2,1)S(1)} all-to-all(bf16[16,80,384]{2,1,0:T(8,128)(2,1)S(1)} %pad_maximum_fusion.1), channel_id=1, replica_groups=mesh['group'=2,'dp'=16] {'dp'}, dimensions={0} | all-to-all | bytes 1966080 | tf_op jit(solution)/shard_map/all_to_all | solution.py:693
  432.4 6.2 %adam.1 = (f32[576,768]{1,0:T(8,128)}, f32[576,768]{1,0:T(8,128)}, f32[576,768]{1,0:T(8,128)}) custom-call(f32[2]{0:T(128)} %pad_maximum_fusion.5.scal_ref, bf16[4,2,2,80,384]{4,3,2,1,0:T(8,128)(2,1)} %bitcast.86, bf16[4,2,2,80,384]{4,3,2,1,0:T(8,128)(2,1)} %bitcast.90, f32[576,768]{1,0:T(8,128)} %w_ref.1, f32[576,768]{1,0:T(8,128)} %m_ref.1, f32[576,768]{1,0:T(8,128)} %v_ref.1), custom_call_target="tpu_custom_call" | custom-call | tf_op jit(solution)/shard_map/adam/pallas_call | solution.py:563
  (173 shorter events, 80.6 us)
Async XLA Ops:
  2.0 29.9 %collective-permute-start.1 = (bf16[208,768]{1,0:T(8,128)(2,1)S(1)}, bf16[208,768]{1,0:T(8,128)(2,1)S(1)}, u32[]{:S(2)}, u32[]{:S(2)}) collective-permute-start(bf16[208,768]{1,0:T(8,128)(2,1)S(1)} %get-tuple-element.170), channel_id=1, source_target_pairs={{0,8},{1,9},{2,10},{3,11},{4,12},{5,13},{6,14},{7,15},{8,0},{9,1},... | collective-permute-start | bytes 958472 | tf_op jit(solution)/shard_map/ppermute | solution.py:627
  6.1 25.8 %collective-permute-start = (bf16[208,768]{1,0:T(8,128)(2,1)S(1)}, bf16[208,768]{1,0:T(8,128)(2,1)S(1)}, u32[]{:S(2)}, u32[]{:S(2)}) collective-permute-start(bf16[208,768]{1,0:T(8,128)(2,1)S(1)} %get-tuple-element.170), channel_id=1, source_target_pairs={{0,4},{1,5},{2,6},{3,7},{4,8},{5,9},{6,10},{7,11},{8,12},{9,13},{1... | collective-permute-start | bytes 958472 | tf_op jit(solution)/shard_map/ppermute | solution.py:627
  7.6 24.3 %collective-permute-start.2 = (bf16[208,768]{1,0:T(8,128)(2,1)S(1)}, bf16[208,768]{1,0:T(8,128)(2,1)S(1)}, u32[]{:S(2)}, u32[]{:S(2)}) collective-permute-start(bf16[208,768]{1,0:T(8,128)(2,1)S(1)} %get-tuple-element.170), channel_id=1, source_target_pairs={{0,12},{1,13},{2,14},{3,15},{4,0},{5,1},{6,2},{7,3},{8,4},{9,5},{1... | collective-permute-start | bytes 958472 | tf_op jit(solution)/shard_map/ppermute | solution.py:627
  9.9 18.9 %collective-permute-start.3 = (bf16[80,768]{1,0:T(8,128)(2,1)S(1)}, bf16[80,768]{1,0:T(8,128)(2,1)S(1)}, u32[]{:S(2)}, u32[]{:S(2)}) collective-permute-start(bf16[80,768]{1,0:T(8,128)(2,1)S(1)} %get-tuple-element.168), channel_id=1, source_target_pairs={{0,1},{1,0},{2,3},{3,2},{4,5},{5,4},{6,7},{7,6},{8,9},{9,8},{10,11... | collective-permute-start | bytes 368648 | tf_op jit(solution)/shard_map/ppermute | solution.py:622
  35.1 17.5 %collective-permute-start.5 = (bf16[4,208,768]{2,1,0:T(8,128)(2,1)S(1)}, bf16[4,208,768]{2,1,0:T(8,128)(2,1)S(1)}, u32[]{:S(2)}, u32[]{:S(2)}) collective-permute-start(bf16[4,208,768]{2,1,0:T(8,128)(2,1)S(1)} %pad_maximum_fusion), channel_id=1, source_target_pairs={{0,1},{1,0},{2,3},{3,2},{4,5},{5,4},{6,7},{7,6},{8,9},{9,8},{10,11... | collective-permute-start | bytes 3833864 | tf_op jit(solution)/shard_map/ppermute | solution.py:622
  52.7 32.3 %collective-permute-start.6 = (bf16[8,208,768]{2,1,0:T(8,128)(2,1)S(1)}, bf16[8,208,768]{2,1,0:T(8,128)(2,1)}, u32[]{:S(2)}, u32[]{:S(2)}) collective-permute-start(bf16[8,208,768]{2,1,0:T(8,128)(2,1)S(1)} %constant_dynamic-update-slice_fusion.rest_0_), channel_id=1, source_target_pairs={{0,2},{1,3},{2,0},{3,1},{4,6},{5,7},{6,4},{7,5},{8,10},{9,11},{10,... | collective-permute-start | bytes 7667720 | tf_op jit(solution)/shard_map/ppermute | solution.py:622
  56.0 29.8 %collective-permute-start.7 = (bf16[4,80,768]{2,1,0:T(8,128)(2,1)S(1)}, bf16[4,80,768]{2,1,0:T(8,128)(2,1)S(1)}, u32[]{:S(2)}, u32[]{:S(2)}) collective-permute-start(bf16[4,80,768]{2,1,0:T(8,128)(2,1)S(1)} %pad_maximum_fusion.3), channel_id=1, source_target_pairs={{0,4},{1,5},{2,6},{3,7},{4,8},{5,9},{6,10},{7,11},{8,12},{9,13},{1... | collective-permute-start | bytes 1474568 | tf_op jit(solution)/shard_map/ppermute | solution.py:627
  56.0 31.0 %collective-permute-start.8 = (bf16[4,80,768]{2,1,0:T(8,128)(2,1)S(1)}, bf16[4,80,768]{2,1,0:T(8,128)(2,1)S(1)}, u32[]{:S(2)}, u32[]{:S(2)}) collective-permute-start(bf16[4,80,768]{2,1,0:T(8,128)(2,1)S(1)} %pad_maximum_fusion.3), channel_id=1, source_target_pairs={{0,8},{1,9},{2,10},{3,11},{4,12},{5,13},{6,14},{7,15},{8,0},{9,1},... | collective-permute-start | bytes 1474568 | tf_op jit(solution)/shard_map/ppermute | solution.py:627
  56.0 31.8 %collective-permute-start.9 = (bf16[4,80,768]{2,1,0:T(8,128)(2,1)S(1)}, bf16[4,80,768]{2,1,0:T(8,128)(2,1)S(1)}, u32[]{:S(2)}, u32[]{:S(2)}) collective-permute-start(bf16[4,80,768]{2,1,0:T(8,128)(2,1)S(1)} %pad_maximum_fusion.3), channel_id=1, source_target_pairs={{0,12},{1,13},{2,14},{3,15},{4,0},{5,1},{6,2},{7,3},{8,4},{9,5},{1... | collective-permute-start | bytes 1474568 | tf_op jit(solution)/shard_map/ppermute | solution.py:627
  59.9 33.2 %collective-permute-start.10 = (bf16[8,208,768]{2,1,0:T(8,128)(2,1)S(1)}, bf16[8,208,768]{2,1,0:T(8,128)(2,1)}, u32[]{:S(2)}, u32[]{:S(2)}) collective-permute-start(bf16[8,208,768]{2,1,0:T(8,128)(2,1)S(1)} %constant_dynamic-update-slice_fusion.rest_0_), channel_id=1, source_target_pairs={{0,16},{16,0},{1,17},{17,1},{2,18},{18,2},{3,19},{19,3},{4,20},{20... | collective-permute-start | bytes 7667720 | tf_op jit(solution)/shard_map/ppermute | solution.py:646
  85.1 8.0 %collective-permute-start.11 = (bf16[8,208,768]{2,1,0:T(8,128)(2,1)}, bf16[8,208,768]{2,1,0:T(8,128)(2,1)}, u32[]{:S(2)}, u32[]{:S(2)}) collective-permute-start(bf16[8,208,768]{2,1,0:T(8,128)(2,1)} %collective-permute-done.6.rest_1_), channel_id=1, source_target_pairs={{0,16},{16,0},{1,17},{17,1},{2,18},{18,2},{3,19},{19,3},{4,20},{20... | collective-permute-start | bytes 7667720 | tf_op jit(solution)/shard_map/ppermute | solution.py:646
  203.1 10.5 %collective-permute-start.13 = (bf16[6,576,768]{2,1,0:T(8,128)(2,1)}, bf16[6,576,768]{2,1,0:T(8,128)(2,1)}, u32[]{:S(2)}, u32[]{:S(2)}) collective-permute-start(bf16[6,576,768]{2,1,0:T(8,128)(2,1)} %get-tuple-element.90), channel_id=1, source_target_pairs={{0,16},{16,0},{1,17},{17,1},{2,18},{18,2},{3,19},{19,3},{4,20},{20... | collective-permute-start | bytes 15925256 | tf_op jit(solution)/shard_map/ppermute | solution.py:779
  220.3 32.2 %collective-permute-start.14 = (bf16[2,6,288,384]{3,2,1,0:T(8,128)(2,1)}, bf16[2,6,288,384]{3,2,1,0:T(8,128)(2,1)S(1)}, u32[]{:S(2)}, u32[]{:S(2)}) collective-permute-start(bf16[2,6,288,384]{3,2,1,0:T(8,128)(2,1)} %fold.6), channel_id=1, source_target_pairs={{0,1},{1,0},{2,3},{3,2},{4,5},{5,4},{6,7},{7,6},{8,9},{9,8},{10,11... | collective-permute-start | bytes 7962632 | tf_op jit(solution)/shard_map/ppermute | solution.py:622
  259.9 18.9 %collective-permute-start.15 = (bf16[1,6,288,384]{3,2,1,0:T(8,128)(2,1)}, bf16[1,6,288,384]{3,2,1,0:T(8,128)(2,1)S(1)}, u32[]{:S(2)}, u32[]{:S(2)}) collective-permute-start(bf16[1,6,288,384]{3,2,1,0:T(8,128)(2,1)} %fold.7), channel_id=1, source_target_pairs={{0,2},{1,3},{2,0},{3,1},{4,6},{5,7},{6,4},{7,5},{8,10},{9,11},{10,... | collective-permute-start | bytes 3981320 | tf_op jit(solution)/shard_map/ppermute | solution.py:622
  295.3 10.1 %collective-permute-start.16 = (bf16[2,576,768]{2,1,0:T(8,128)(2,1)}, bf16[2,576,768]{2,1,0:T(8,128)(2,1)S(1)}, u32[]{:S(2)}, u32[]{:S(2)}) collective-permute-start(bf16[2,576,768]{2,1,0:T(8,128)(2,1)} %get-tuple-element.129), channel_id=1, source_target_pairs={{0,16},{16,0},{1,17},{17,1},{2,18},{18,2},{3,19},{19,3},{4,20},{20... | collective-permute-start | bytes 5308424 | tf_op jit(solution)/shard_map/ppermute | solution.py:805
  309.8 43.1 %collective-permute-start.17 = (bf16[2,2,288,384]{3,2,1,0:T(8,128)(2,1)}, bf16[2,2,288,384]{3,2,1,0:T(8,128)(2,1)S(1)}, u32[]{:S(2)}, u32[]{:S(2)}) collective-permute-start(bf16[2,2,288,384]{3,2,1,0:T(8,128)(2,1)} %fold.9), channel_id=1, source_target_pairs={{0,1},{1,0},{2,3},{3,2},{4,5},{5,4},{6,7},{7,6},{8,9},{9,8},{10,11... | collective-permute-start | bytes 2654216 | tf_op jit(solution)/shard_map/ppermute | solution.py:622
  310.9 22.0 %collective-permute-start.20 = (bf16[6,72,384]{2,1,0:T(8,128)(2,1)}, bf16[6,72,384]{2,1,0:T(8,128)(2,1)S(1)}, u32[]{:S(2)}, u32[]{:S(2)}) collective-permute-start(bf16[6,72,384]{2,1,0:T(8,128)(2,1)} %get-tuple-element.158), channel_id=1, source_target_pairs={{0,12},{1,13},{2,14},{3,15},{4,0},{5,1},{6,2},{7,3},{8,4},{9,5},{1... | collective-permute-start | bytes 995336 | tf_op jit(solution)/shard_map/ppermute | solution.py:627
  324.3 28.6 %collective-permute-start.19 = (bf16[6,72,384]{2,1,0:T(8,128)(2,1)S(1)}, bf16[6,72,384]{2,1,0:T(8,128)(2,1)S(1)}, u32[]{:S(2)}, u32[]{:S(2)}) collective-permute-start(bf16[6,72,384]{2,1,0:T(8,128)(2,1)S(1)} %get-tuple-element.159), channel_id=1, source_target_pairs={{0,8},{1,9},{2,10},{3,11},{4,12},{5,13},{6,14},{7,15},{8,0},{9,1},... | collective-permute-start | bytes 995336 | tf_op jit(solution)/shard_map/ppermute | solution.py:627
  324.3 28.6 %collective-permute-start.18 = (bf16[6,72,384]{2,1,0:T(8,128)(2,1)S(1)}, bf16[6,72,384]{2,1,0:T(8,128)(2,1)S(1)}, u32[]{:S(2)}, u32[]{:S(2)}) collective-permute-start(bf16[6,72,384]{2,1,0:T(8,128)(2,1)S(1)} %get-tuple-element.160), channel_id=1, source_target_pairs={{0,4},{1,5},{2,6},{3,7},{4,8},{5,9},{6,10},{7,11},{8,12},{9,13},{1... | collective-permute-start | bytes 995336 | tf_op jit(solution)/shard_map/ppermute | solution.py:627
  357.1 23.2 %collective-permute-start.21 = (bf16[1,2,288,384]{3,2,1,0:T(8,128)(2,1)}, bf16[1,2,288,384]{3,2,1,0:T(8,128)(2,1)S(1)}, u32[]{:S(2)}, u32[]{:S(2)}) collective-permute-start(bf16[1,2,288,384]{3,2,1,0:T(8,128)(2,1)} %fold.10), channel_id=1, source_target_pairs={{0,2},{1,3},{2,0},{3,1},{4,6},{5,7},{6,4},{7,5},{8,10},{9,11},{10,... | collective-permute-start | bytes 1327112 | tf_op jit(solution)/shard_map/ppermute | solution.py:622
  374.0 6.3 %collective-permute-start.29 = (f32[14,768]{1,0:T(8,128)S(1)}, f32[14,768]{1,0:T(8,128)S(1)}, u32[]{:S(2)}, u32[]{:S(2)}) collective-permute-start(f32[14,768]{1,0:T(8,128)S(1)} %add.200), channel_id=1, source_target_pairs={{0,8},{1,9},{2,10},{3,11},{4,12},{5,13},{6,14},{7,15},{8,0},{9,1},... | collective-permute-start | bytes 129032 | tf_op jit(solution)/shard_map/ppermute | solution.py:611
  385.1 6.8 %collective-permute-start.22 = (bf16[2,72,384]{2,1,0:T(8,128)(2,1)S(1)}, bf16[2,72,384]{2,1,0:T(8,128)(2,1)S(1)}, u32[]{:S(2)}, u32[]{:S(2)}) collective-permute-start(bf16[2,72,384]{2,1,0:T(8,128)(2,1)S(1)} %get-tuple-element.164), channel_id=1, source_target_pairs={{0,4},{1,5},{2,6},{3,7},{4,8},{5,9},{6,10},{7,11},{8,12},{9,13},{1... | collective-permute-start | bytes 331784 | tf_op jit(solution)/shard_map/ppermute | solution.py:627
  385.4 7.7 %collective-permute-start.24 = (bf16[2,72,384]{2,1,0:T(8,128)(2,1)S(1)}, bf16[2,72,384]{2,1,0:T(8,128)(2,1)S(1)}, u32[]{:S(2)}, u32[]{:S(2)}) collective-permute-start(bf16[2,72,384]{2,1,0:T(8,128)(2,1)S(1)} %get-tuple-element.165), channel_id=1, source_target_pairs={{0,12},{1,13},{2,14},{3,15},{4,0},{5,1},{6,2},{7,3},{8,4},{9,5},{1... | collective-permute-start | bytes 331784 | tf_op jit(solution)/shard_map/ppermute | solution.py:627
  389.0 6.5 %collective-permute-start.23 = (bf16[2,72,384]{2,1,0:T(8,128)(2,1)S(1)}, bf16[2,72,384]{2,1,0:T(8,128)(2,1)S(1)}, u32[]{:S(2)}, u32[]{:S(2)}) collective-permute-start(bf16[2,72,384]{2,1,0:T(8,128)(2,1)S(1)} %get-tuple-element.166), channel_id=1, source_target_pairs={{0,8},{1,9},{2,10},{3,11},{4,12},{5,13},{6,14},{7,15},{8,0},{9,1},... | collective-permute-start | bytes 331784 | tf_op jit(solution)/shard_map/ppermute | solution.py:627
  (26 other events, 287.8 us)
